TPU v7x, 256 devices: a whole 4x4x8 slice. The times are simulated.
256 devices in a mesh: inner: 4 (over y), outer: 64 (over z, x, core).
Axes of the slice: x: 4, y: 4, z: 8, core: 2. Of those that a mesh axis runs over, the one named last changes fastest.
Arguments:
- queries: bfloat16 [32768, 640], P(('inner', 'outer')), may hold values from -6 to 6
- keys: bfloat16 [32768, 128], P(('inner', 'outer')), may hold values from -6 to 6
- values: bfloat16 [32768, 128], P(('inner', 'outer')), may hold values from -6 to 6
- attention_out: bfloat16 [32768, 640], P(('inner', 'outer')), may hold values from -4 to 4
- output_grad: bfloat16 [32768, 640], P(('inner', 'outer')), may hold values from -6 to 6
- log_norm: float32 [5, 32768], P(None, ('inner', 'outer')), may hold values from 3 to 6
- layer_input: bfloat16 [32768, 5120], P(('inner', 'outer'))
- doc_start: int32 [32768], P(('inner', 'outer')), may hold values from 0 to 32767, as said below
- visible_blocks: int32 [256, 5], P(('inner', 'outer')), may hold values from -1 to 255, as said below
Outputs:
- projection_grad: float32 [5120, 256], P(('inner', 'outer'))
- query_grad: bfloat16 [32768, 640], P(('inner', 'outer'))
Inputs may be any that keep to these rules, and one draw needn't show every extreme that they name: doc_start[t] is the first position of the document holding position t: it is at most t, equal over one document, and a document begins where it changes. A document has at most 512 positions and one has exactly 512. `visible_blocks`: row i lists in ascending order the key blocks from the block that holds doc_start[i * 128] up to block i, followed by -1 in the slots left over; some row has no -1.
All inputs are finite; a program needn't handle non-finite values.
Results may differ from a plain program's by a relative error of at most 0.0057.
Values may be sent and summed in bfloat16 or wider, within the bound.
A program may use at most 64 MiB of HBM per device.

v0:
```python
import jax
import jax.numpy as jnp
from jax import lax
from jax.sharding import PartitionSpec as P

D = 5120
HD = 128
VIS = 5


def passed_along(value, axis, steps):
    count = lax.axis_size(axis)
    leading, last = (max(0, -steps), min(count, count - steps))
    return lax.ppermute(value, axis, [(source, source + steps) for source in range(leading, last)])


def passed_along_2(value, axis, by):
    size = lax.axis_size(axis)
    return lax.ppermute(value, axis, [(i, (i + by) % size) for i in range(size)])


def block_terms(
    query_heads, grad_heads, row_delta, log_norm, allowed, key_rows, value_rows, inv_scale
):
    scores = (
        jnp.einsum("thd,ud->htu", query_heads, key_rows, preferred_element_type=jnp.float32)
        * inv_scale
    )
    prob_full = jnp.where(allowed[None], jnp.exp(scores - log_norm[:, :, None]), jnp.float32(0.0))
    prob_half = prob_full.astype(jnp.bfloat16)
    prob_grad = jnp.einsum(
        "thd,ud->htu", grad_heads, value_rows, preferred_element_type=jnp.float32
    )
    score_grad = (prob_full * (prob_grad - row_delta[:, :, None]) * inv_scale).astype(jnp.bfloat16)
    query_part = jnp.einsum("htu,ud->thd", score_grad, key_rows, preferred_element_type=jnp.float32)
    key_part = jnp.einsum(
        "htu,thd->ud", score_grad, query_heads, preferred_element_type=jnp.float32
    )
    value_part = jnp.einsum(
        "htu,thd->ud", prob_half, grad_heads, preferred_element_type=jnp.float32
    )
    return (query_part, key_part, value_part)


def on_device(
    queries,
    keys,
    values,
    attention_out,
    output_grad,
    log_norm,
    layer_input,
    doc_start,
    visible_blocks,
):
    block_rows = queries.shape[0]
    head_dim = keys.shape[1]
    num_heads = log_norm.shape[0]
    my_block = lax.axis_index(("inner", "outer"))
    query_heads = queries.reshape(block_rows, num_heads, head_dim)
    grad_heads = output_grad.reshape(block_rows, num_heads, head_dim)
    out_heads = attention_out.reshape(block_rows, num_heads, head_dim)
    row_delta = jnp.sum(grad_heads.astype(jnp.float32) * out_heads.astype(jnp.float32), axis=2).T
    inv_scale = 1.0 / jnp.sqrt(jnp.float32(head_dim))
    query_pos = my_block * block_rows + jnp.arange(block_rows, dtype=jnp.int32)
    listed = visible_blocks[0]
    key_value = (keys, values)
    carry_key = jnp.zeros((block_rows, head_dim), jnp.float32)
    carry_value = jnp.zeros((block_rows, head_dim), jnp.float32)
    query_sum = jnp.zeros((block_rows, num_heads, head_dim), jnp.float32)
    for cycle_step in range(VIS):
        if cycle_step > 0:
            key_value = passed_along((key_value[0], key_value[1]), ("inner", "outer"), 1)
            carry_key, carry_value = passed_along_2((carry_key, carry_value), ("inner", "outer"), 1)
        key_block = my_block - cycle_step
        in_list = jnp.any(listed == key_block) & (key_block >= 0)
        key_pos = key_block * block_rows + jnp.arange(block_rows, dtype=jnp.int32)
        allowed = (
            in_list
            & (key_pos[None, :] >= doc_start[:, None])
            & (key_pos[None, :] <= query_pos[:, None])
        )
        key_rows, value_rows = key_value
        query_part, key_part, value_part = block_terms(
            query_heads, grad_heads, row_delta, log_norm, allowed, key_rows, value_rows, inv_scale
        )
        query_sum = query_sum + query_part
        carry_key = carry_key + key_part
        carry_value = carry_value + value_part
    carry_key, carry_value = (
        passed_along_2(carry_key.astype(jnp.bfloat16), ("inner", "outer"), -(VIS - 1)).astype(
            carry_key.dtype
        ),
        passed_along_2(carry_value.astype(jnp.bfloat16), ("inner", "outer"), -(VIS - 1)).astype(
            carry_value.dtype
        ),
    )
    query_grad = query_sum.reshape(block_rows, num_heads * head_dim).astype(jnp.bfloat16)
    all_grads = jnp.concatenate(
        [carry_key.astype(jnp.bfloat16), carry_value.astype(jnp.bfloat16)], axis=1
    )
    weight_sum = lax.psum_scatter(
        lax.dot_general(
            layer_input, all_grads, (((0,), (0,)), ((), ())), preferred_element_type=jnp.float32
        ),
        ("inner", "outer"),
        scatter_dimension=0,
        tiled=True,
    )
    square_total = lax.psum(jnp.sum(weight_sum * weight_sum), ("inner", "outer"))
    limit = jnp.sqrt(jnp.float32(D * 2 * HD))
    clip_factor = jnp.minimum(jnp.float32(1.0), limit / (jnp.sqrt(square_total) + 1e-06))
    return (weight_sum * clip_factor, query_grad)


def solution(mesh):
    return jax.shard_map(
        on_device,
        mesh=mesh,
        in_specs=(
            P(("inner", "outer"), None),
            P(("inner", "outer"), None),
            P(("inner", "outer"), None),
            P(("inner", "outer"), None),
            P(("inner", "outer"), None),
            P(None, ("inner", "outer")),
            P(("inner", "outer"), None),
            P(("inner", "outer")),
            P(("inner", "outer"), None),
        ),
        out_specs=(P(("inner", "outer"), None), P(("inner", "outer"), None)),
        check_vma=False,
    )
```

profile of v0, /device:TPU:1, one launch (start us, length us, event | category | flops | bytes accessed | tf_op | source)
XLA Modules:
  0.0 442.9 jit_solution(15319395701004665441)
XLA Ops:
  7.2 4.6 %collective-permute-start.2 = (bf16[128,128]{1,0:T(8,128)(2,1)}, bf16[128,128]{1,0:T(8,128)(2,1)S(1)}, u32[]{:S(2)}, u32[]{:S(2)}) collective-permute-start(bf16[128,128]{1,0:T(8,128)(2,1)} %param.11), channel_id=1, source_target_pairs={{0,1},{1,2},{2,3},{3,4},{4,5},{5,6},{6,7},{7,8},{8,9},{9,10},{10,1... | collective-permute-start | bytes 98312 | tf_op jit(solution)/shard_map/ppermute | solution.py:14
  11.9 1.9 collective-permute-start.1
  13.8 1.4 compare_reduce_fusion
  15.3 1.1 copy.58
  16.3 1.1 copy.62
  17.4 1.1 copy.60
  21.8 0.8 compare_and_fusion
  22.6 1.0 fusion.15
  23.6 1.0 fusion.36
  24.7 1.7 collective-permute-start
  26.7 3.2 collective-permute-start.5
  29.9 1.9 collective-permute-start.4
  31.9 0.9 fusion.16
  33.0 0.9 fusion.17
  34.4 2.2 collective-permute-start.3
  36.6 1.9 collective-permute-start.7
  39.2 2.0 collective-permute-start.14
  41.2 1.9 collective-permute-start.8
  43.5 3.5 collective-permute-start.10
  47.5 1.9 collective-permute-start.11
  49.4 3.8 collective-permute-start.6
  54.5 2.4 collective-permute-start.9
  57.2 1.0 collective-permute-start.16
  58.2 1.7 collective-permute-done.9
  60.0 2.4 collective-permute-start.12
  62.4 5.9 %collective-permute-start.17 = (bf16[128,128]{1,0:T(8,128)(2,1)S(1)}, bf16[128,128]{1,0:T(8,128)(2,1)S(1)}, u32[]{:S(2)}, u32[]{:S(2)}) collective-permute-start(bf16[128,128]{1,0:T(8,128)(2,1)S(1)} %add_convert_fusion), channel_id=1, source_target_pairs={{0,252},{1,253},{2,254},{3,255},{4,0},{5,1},{6,2},{7,3},{8,4},{9,5... | collective-permute-start | bytes 98312 | tf_op jit(solution)/shard_map/ppermute | solution.py:19
  68.3 1.0 collective-permute-done.17
  69.3 3.2 convolution_bitcast_fusion
  73.8 279.6 %all-reduce.3.cloned.1.call-done = f32[5120,256]{0,1:T(8,128)} async-done(((f32[5120,256]{0,1:T(8,128)}), f32[5120,256]{0,1:T(8,128)}) %all-reduce.3.cloned.1.call-update) | async-done | bytes 5242896
  353.3 1.7 multiply_reduce_fusion
  355.8 77.7 %psum.7 = f32[]{:T(128)} all-reduce(f32[]{:T(128)} %multiply_reduce_fusion), channel_id=1, replica_groups=mesh['inner'=4,'outer'=64] {'inner','outer'}, use_global_device_ids=true, to_apply=%region_8.9 | all-reduce | flops 1 | bytes 8 | tf_op jit(solution)/shard_map/psum | solution.py:110
  434.2 1.1 dynamic-slice_multiply_fusion
  (59 shorter events, 7.0 us)
Async XLA Ops:
  7.2 62.2 %copy-start = (bf16[128,5120]{1,0:T(8,128)(2,1)S(1)}, bf16[128,5120]{1,0:T(8,128)(2,1)}, u32[]{:S(2)}) copy-start(bf16[128,5120]{1,0:T(8,128)(2,1)} %param.15) | copy-start | bytes 3932164
  7.2 35.9 %copy-start.2 = (f32[5,128]{1,0:T(8,128)S(1)}, f32[5,128]{1,0:T(8,128)}, u32[]{:S(2)}) copy-start(f32[5,128]{1,0:T(8,128)} %param.14) | copy-start | bytes 7684
  7.2 346.1 %all-reduce.3.cloned.1.call-start = ((), (), s32[]{:S(2)}) async-start(), calls=%async_computation | async-start | bytes 10485760
  7.2 19.5 %collective-permute-start.2 = (bf16[128,128]{1,0:T(8,128)(2,1)}, bf16[128,128]{1,0:T(8,128)(2,1)S(1)}, u32[]{:S(2)}, u32[]{:S(2)}) collective-permute-start(bf16[128,128]{1,0:T(8,128)(2,1)} %param.11), channel_id=1, source_target_pairs={{0,1},{1,2},{2,3},{3,4},{4,5},{5,6},{6,7},{7,8},{8,9},{9,10},{10,1... | collective-permute-start | bytes 98312 | tf_op jit(solution)/shard_map/ppermute | solution.py:14
  11.9 18.0 %collective-permute-start.1 = (bf16[128,128]{1,0:T(8,128)(2,1)}, bf16[128,128]{1,0:T(8,128)(2,1)S(1)}, u32[]{:S(2)}, u32[]{:S(2)}) collective-permute-start(bf16[128,128]{1,0:T(8,128)(2,1)} %param.10), channel_id=1, source_target_pairs={{0,1},{1,2},{2,3},{3,4},{4,5},{5,6},{6,7},{7,8},{8,9},{9,10},{10,1... | collective-permute-start | bytes 98312 | tf_op jit(solution)/shard_map/ppermute | solution.py:14
  24.7 9.2 %collective-permute-start = (f32[128,128]{1,0:T(8,128)S(1)}, f32[128,128]{1,0:T(8,128)S(1)}, u32[]{:S(2)}, u32[]{:S(2)}) collective-permute-start(f32[128,128]{1,0:T(8,128)S(1)} %convolution_bitcast_fusion.15), channel_id=1, source_target_pairs={{0,1},{1,2},{2,3},{3,4},{4,5},{5,6},{6,7},{7,8},{8,9},{9,10},{10,1... | collective-permute-start | bytes 196616 | tf_op jit(solution)/shard_map/ppermute | solution.py:19
  26.6 12.3 %collective-permute-start.13 = (f32[128,128]{1,0:T(8,128)S(1)}, f32[128,128]{1,0:T(8,128)S(1)}, u32[]{:S(2)}, u32[]{:S(2)}) collective-permute-start(f32[128,128]{1,0:T(8,128)S(1)} %convolution_bitcast_fusion.10), channel_id=1, source_target_pairs={{0,1},{1,2},{2,3},{3,4},{4,5},{5,6},{6,7},{7,8},{8,9},{9,10},{10,1... | collective-permute-start | bytes 196616 | tf_op jit(solution)/shard_map/ppermute | solution.py:19
  26.7 11.8 %collective-permute-start.5 = (bf16[128,128]{1,0:T(8,128)(2,1)S(1)}, bf16[128,128]{1,0:T(8,128)(2,1)S(1)}, u32[]{:S(2)}, u32[]{:S(2)}) collective-permute-start(bf16[128,128]{1,0:T(8,128)(2,1)S(1)} %collective-permute-done.2), channel_id=1, source_target_pairs={{0,1},{1,2},{2,3},{3,4},{4,5},{5,6},{6,7},{7,8},{8,9},{9,10},{10,1... | collective-permute-start | bytes 98312 | tf_op jit(solution)/shard_map/ppermute | solution.py:14
  29.9 3.1 collective-permute-start.4
  34.4 15.0 %collective-permute-start.3 = (f32[128,128]{1,0:T(8,128)S(1)}, f32[128,128]{1,0:T(8,128)S(1)}, u32[]{:S(2)}, u32[]{:S(2)}) collective-permute-start(f32[128,128]{1,0:T(8,128)S(1)} %fusion.41), channel_id=1, source_target_pairs={{0,1},{1,2},{2,3},{3,4},{4,5},{5,6},{6,7},{7,8},{8,9},{9,10},{10,1... | collective-permute-start | bytes 196616 | tf_op jit(solution)/shard_map/ppermute | solution.py:19
  36.6 6.5 %collective-permute-start.7 = (bf16[128,128]{1,0:T(8,128)(2,1)S(1)}, bf16[128,128]{1,0:T(8,128)(2,1)S(1)}, u32[]{:S(2)}, u32[]{:S(2)}) collective-permute-start(bf16[128,128]{1,0:T(8,128)(2,1)S(1)} %collective-permute-done.4), channel_id=1, source_target_pairs={{0,1},{1,2},{2,3},{3,4},{4,5},{5,6},{6,7},{7,8},{8,9},{9,10},{10,1... | collective-permute-start | bytes 98312 | tf_op jit(solution)/shard_map/ppermute | solution.py:14
  39.2 14.7 %collective-permute-start.14 = (f32[128,128]{1,0:T(8,128)S(1)}, f32[128,128]{1,0:T(8,128)S(1)}, u32[]{:S(2)}, u32[]{:S(2)}) collective-permute-start(f32[128,128]{1,0:T(8,128)S(1)} %fusion.42), channel_id=1, source_target_pairs={{0,1},{1,2},{2,3},{3,4},{4,5},{5,6},{6,7},{7,8},{8,9},{9,10},{10,1... | collective-permute-start | bytes 196616 | tf_op jit(solution)/shard_map/ppermute | solution.py:19
  41.2 5.9 %collective-permute-start.8 = (bf16[128,128]{1,0:T(8,128)(2,1)S(1)}, bf16[128,128]{1,0:T(8,128)(2,1)S(1)}, u32[]{:S(2)}, u32[]{:S(2)}) collective-permute-start(bf16[128,128]{1,0:T(8,128)(2,1)S(1)} %collective-permute-done.5), channel_id=1, source_target_pairs={{0,1},{1,2},{2,3},{3,4},{4,5},{5,6},{6,7},{7,8},{8,9},{9,10},{10,1... | collective-permute-start | bytes 98312 | tf_op jit(solution)/shard_map/ppermute | solution.py:14
  43.5 9.7 %collective-permute-start.10 = (bf16[128,128]{1,0:T(8,128)(2,1)S(1)}, bf16[128,128]{1,0:T(8,128)(2,1)S(1)}, u32[]{:S(2)}, u32[]{:S(2)}) collective-permute-start(bf16[128,128]{1,0:T(8,128)(2,1)S(1)} %collective-permute-done.7), channel_id=1, source_target_pairs={{0,1},{1,2},{2,3},{3,4},{4,5},{5,6},{6,7},{7,8},{8,9},{9,10},{10,1... | collective-permute-start | bytes 98312 | tf_op jit(solution)/shard_map/ppermute | solution.py:14
  47.5 6.0 %collective-permute-start.11 = (bf16[128,128]{1,0:T(8,128)(2,1)S(1)}, bf16[128,128]{1,0:T(8,128)(2,1)S(1)}, u32[]{:S(2)}, u32[]{:S(2)}) collective-permute-start(bf16[128,128]{1,0:T(8,128)(2,1)S(1)} %collective-permute-done.8), channel_id=1, source_target_pairs={{0,1},{1,2},{2,3},{3,4},{4,5},{5,6},{6,7},{7,8},{8,9},{9,10},{10,1... | collective-permute-start | bytes 98312 | tf_op jit(solution)/shard_map/ppermute | solution.py:14
  49.4 5.1 %collective-permute-start.6 = (f32[128,128]{1,0:T(8,128)S(1)}, f32[128,128]{1,0:T(8,128)S(1)}, u32[]{:S(2)}, u32[]{:S(2)}) collective-permute-start(f32[128,128]{1,0:T(8,128)S(1)} %add.120), channel_id=1, source_target_pairs={{0,1},{1,2},{2,3},{3,4},{4,5},{5,6},{6,7},{7,8},{8,9},{9,10},{10,1... | collective-permute-start | bytes 196616 | tf_op jit(solution)/shard_map/ppermute | solution.py:19
  53.9 3.3 collective-permute-start.15
  54.5 5.4 %collective-permute-start.9 = (f32[128,128]{1,0:T(8,128)S(1)}, f32[128,128]{1,0:T(8,128)S(1)}, u32[]{:S(2)}, u32[]{:S(2)}) collective-permute-start(f32[128,128]{1,0:T(8,128)S(1)} %add.123), channel_id=1, source_target_pairs={{0,1},{1,2},{2,3},{3,4},{4,5},{5,6},{6,7},{7,8},{8,9},{9,10},{10,1... | collective-permute-start | bytes 196616 | tf_op jit(solution)/shard_map/ppermute | solution.py:19
  57.2 5.2 %collective-permute-start.16 = (f32[128,128]{1,0:T(8,128)S(1)}, f32[128,128]{1,0:T(8,128)S(1)}, u32[]{:S(2)}, u32[]{:S(2)}) collective-permute-start(f32[128,128]{1,0:T(8,128)S(1)} %add.129), channel_id=1, source_target_pairs={{0,1},{1,2},{2,3},{3,4},{4,5},{5,6},{6,7},{7,8},{8,9},{9,10},{10,1... | collective-permute-start | bytes 196616 | tf_op jit(solution)/shard_map/ppermute | solution.py:19
  60.0 8.3 %collective-permute-start.12 = (bf16[128,128]{1,0:T(8,128)(2,1)S(1)}, bf16[128,128]{1,0:T(8,128)(2,1)S(1)}, u32[]{:S(2)}, u32[]{:S(2)}) collective-permute-start(bf16[128,128]{1,0:T(8,128)(2,1)S(1)} %add_convert_fusion.1), channel_id=1, source_target_pairs={{0,252},{1,253},{2,254},{3,255},{4,0},{5,1},{6,2},{7,3},{8,4},{9,5... | collective-permute-start | bytes 98312 | tf_op jit(solution)/shard_map/ppermute | solution.py:19
  62.4 10.1 %copy-start.1 = (bf16[128,128]{1,0:T(8,128)(2,1)S(1)}, bf16[128,128]{1,0:T(8,128)(2,1)}, u32[]{:S(2)}) copy-start(bf16[128,128]{1,0:T(8,128)(2,1)} %param.10) | copy-start | bytes 98308
  62.4 6.9 %collective-permute-start.17 = (bf16[128,128]{1,0:T(8,128)(2,1)S(1)}, bf16[128,128]{1,0:T(8,128)(2,1)S(1)}, u32[]{:S(2)}, u32[]{:S(2)}) collective-permute-start(bf16[128,128]{1,0:T(8,128)(2,1)S(1)} %add_convert_fusion), channel_id=1, source_target_pairs={{0,252},{1,253},{2,254},{3,255},{4,0},{5,1},{6,2},{7,3},{8,4},{9,5... | collective-permute-start | bytes 98312 | tf_op jit(solution)/shard_map/ppermute | solution.py:19
Sparse Core Ops, SparseCore 0:
  72.7 280.6 all-reduce.2
where the time goes:
time: 444 us; the launch traced here: 443 us
  waiting for transfers between devices  282 us (64%)
  blocking collectives  77.7 us (18%)
  starting transfers between devices  43.1 us (10%)
  between operations  18.4 us (4%)
  matrix products  11.3 us (3%)
  other arithmetic  5.07 us (1%)
  local copies, waits for them, and re-layouts  4.76 us (1%)
    unnamed x2, waiting for transfers between devices  280 us
    psum x1, blocking collectives, on_device(): lax.psum(jnp.sum(weight_sum * weight_sum), ('inner', 'outer'))  77.7 us
    ppermute x10, starting transfers between devices, passed_along_2(): lax.ppermute(value, axis, [(i, (i + by) % size) for i in range(size)])  22.1 us
    ppermute x8, starting transfers between devices, passed_along(): lax.ppermute(value, axis, [(source, source + steps) for source in range(l...  21 us
  transfers between devices with their start and end apart: 19, of which 4 were waited for; matrix products, arithmetic and copies ran while one was open for 3% of the time, Pallas kernels for 0%

commit v1 on v0

v1 whole, which is shorter than its diff:
```python
import math

import jax
import jax.numpy as jnp
from jax import lax
from jax.experimental import pallas as pl
from jax.experimental.pallas import tpu as pltpu
from jax.sharding import PartitionSpec as P

D = 5120
HD = 128
HQ = 5
T = 128
Y, Z, X, C = 4, 8, 4, 2
N = Y * Z * X * C
DY = D // Y
DC = DY // C
ROWS = D // N
WIN = 24
FAR = 1.0e9
MESH = pl.DeviceIdType.MESH
f32, bf16 = jnp.float32, jnp.bfloat16
SCALE = 1.0 / math.sqrt(HD)
LOG2E = math.log2(math.e)


def place(y, z, x, c):
    return {"inner": y, "outer": (z * X + x) * C + c}


def dot(a, b, dims):
    return lax.dot_general(a, b, (dims, ((), ())), preferred_element_type=f32)


def kernel(
    q_hbm,
    k_hbm,
    v_hbm,
    o_hbm,
    do_hbm,
    lse_ref,
    x_hbm,
    start_ref,
    vis_ref,
    w_ref,
    dq_ref,
    q_all,
    do_all,
    o_own,
    kbuf,
    vbuf,
    stat,
    ds_buf,
    ret_send,
    ret_recv,
    dq_part,
    dq_recv,
    x_recv,
    xt,
    g_all,
    acc,
    rs_send,
    rs_recv,
    wsum,
    sq1,
    sq2,
    load_sem,
    qx_s,
    qx_r,
    kv_s,
    kv_r,
    ret_s,
    ret_r,
    x_s,
    x_r,
    g_s,
    g_r,
    fwd_s,
    dq_s,
    dq_r,
    rs_s,
    rs_r,
    sq_s,
    sq_r,
):
    y = lax.axis_index("inner")
    outer = lax.axis_index("outer")
    z = outer // (X * C)
    x = (outer // C) % X
    c = outer % C
    other = 1 - c
    block = y * (Z * X * C) + outer
    sib = place(y, z, x, other)
    rs_core = z // (Z // C)
    self_rs = rs_core == c

    def block_at(step):
        b = lax.rem(block + (step + N), N)
        return {"inner": b // (Z * X * C), "outer": lax.rem(b, Z * X * C)}

    def send(src, dst, ssem, rsem, device):
        copy = pltpu.make_async_remote_copy(
            src_ref=src, dst_ref=dst, send_sem=ssem, recv_sem=rsem, device_id=device, device_id_type=MESH
        )
        return copy

    loads = [
        pltpu.make_async_copy(do_hbm, do_all.at[c], load_sem.at[0]),
        pltpu.make_async_copy(o_hbm, o_own, load_sem.at[1]),
        pltpu.make_async_copy(q_hbm, q_all.at[c], load_sem.at[2]),
        pltpu.make_async_copy(k_hbm, kbuf.at[0], load_sem.at[3]),
        pltpu.make_async_copy(v_hbm, vbuf.at[0], load_sem.at[4]),
    ]
    for load in loads:
        load.start()

    barrier = pltpu.get_barrier_semaphore()

    def greet(device):
        pl.semaphore_signal(barrier, inc=1, device_id=device, device_id_type=MESH)

    greet(sib)
    for step in (-4, -2, 2, 4):
        greet(block_at(step))
    for dy in range(1, Y):
        for cc in range(C):
            greet(place(lax.rem(y + dy, Y), z, x, cc))

    def greet_rs(i, _):
        zz, xx = i // X, lax.rem(i, X)

        @pl.when(jnp.logical_not((zz == z) & (xx == x) & self_rs))
        def _():
            greet(place(y, zz, xx, rs_core))

        return 0

    lax.fori_loop(0, Z * X, greet_rs, 0)

    def greet_xy(i, _):
        greet(place(lax.rem(y + i // X, Y), z, lax.rem(x + lax.rem(i, X), X), c))
        return 0

    lax.fori_loop(1, Y * X, greet_xy, 0)

    def greet_zc(i, _):
        greet(place(y, lax.rem(z + i // C, Z), x, lax.rem(c + lax.rem(i, C), C)))
        return 0

    lax.fori_loop(1, Z * C, greet_zc, 0)

    loads[0].wait()
    loads[1].wait()
    for h in range(HQ):
        cols = pl.ds(h * HD, HD)
        prod = do_all[c, :, cols].astype(f32) * o_own[:, cols].astype(f32)
        stat[c, pl.ds(h, 1), :] = jnp.sum(prod.T, axis=0, keepdims=True)
    stat[c, pl.ds(HQ, HQ), :] = lse_ref[...] * LOG2E
    first = start_ref[...].astype(f32)
    for d in range(5):
        kb = block - d
        wanted = jnp.where(kb >= 0, kb, -7)
        hit = jnp.max(jnp.where(vis_ref[...] == wanted, 1.0, 0.0), axis=1, keepdims=True)
        stat[c, pl.ds(10 + d, 1), :] = jnp.where(hit > 0.5, first, FAR)
    stat[c, pl.ds(15, 1), :] = jnp.full((1, T), FAR, f32)

    waits = 1 + 4 + 6 + (Y * X - 1) + (Z * C - 1) + Z * X
    pl.semaphore_wait(barrier, waits - jnp.where(self_rs, 1, 0))

    cp_q = send(q_hbm, q_all.at[c], qx_s.at[0], qx_r.at[0], sib)
    cp_do = send(do_hbm, do_all.at[c], qx_s.at[1], qx_r.at[1], sib)
    cp_st = send(stat.at[c], stat.at[c], qx_s.at[2], qx_r.at[2], sib)
    cp_kv = []
    for j in (1, 2):
        cp_kv.append(send(k_hbm, kbuf.at[j], kv_s.at[2 * j - 2], kv_r.at[2 * j - 2], block_at(2 * j)))
        cp_kv.append(send(v_hbm, vbuf.at[j], kv_s.at[2 * j - 1], kv_r.at[2 * j - 1], block_at(2 * j)))
    for copy in cp_kv:
        copy.start()
    cp_st.start()
    cp_q.start()
    cp_do.start()

    def x_cols(yy, cc):
        return x_hbm.at[:, pl.ds(pl.multiple_of(yy * DY + cc * DC, HD), DC)]

    x_own = pltpu.make_async_copy(x_cols(y, c), x_recv.at[y, pl.ds(pl.multiple_of(c * T, T), T)], load_sem.at[5])
    x_own.start()
    my_rows = x_recv.at[y, pl.ds(pl.multiple_of(c * T, T), T)]
    cp_x = []
    for i, (dy, dc) in enumerate([(0, 1), (1, 0), (3, 0), (1, 1), (3, 1), (2, 0), (2, 1)]):
        yy, cc = lax.rem(y + dy, Y), lax.rem(c + dc, C)
        copy = send(x_cols(yy, cc), my_rows, x_s.at[i], x_r.at[i], place(yy, z, x, cc))
        copy.start()
        cp_x.append(copy)

    for load in loads[2:]:
        load.wait()
    cp_q.wait_recv()
    cp_do.wait_recv()
    cp_st.wait_recv()

    def row(r):
        return jnp.concatenate([stat[0, pl.ds(r, 1), :], stat[1, pl.ds(r, 1), :]], axis=1)

    iota_u = lax.broadcasted_iota(jnp.int32, (T, 2 * T), 0)
    iota_t = lax.broadcasted_iota(jnp.int32, (T, 2 * T), 1)
    pair_first = (block - c) * T
    query_pos = pair_first + iota_t
    own_key = own_value = None
    for j in range(3):
        if j > 0:
            cp_kv[2 * j - 2].wait_recv()
            cp_kv[2 * j - 1].wait_recv()
        key_pos = (block - 2 * j) * T + iota_u
        lows = []
        for i in range(C):
            d0, d1 = i + 2 * j, i - 1 + 2 * j
            at0, at1 = 10 + min(d0, 5), 10 + (d1 if d1 >= 0 else 5)
            lows.append(jnp.where(c == 0, stat[i, pl.ds(at0, 1), :], stat[i, pl.ds(at1, 1), :]))
        low = jnp.concatenate(lows, axis=1)
        allowed = (key_pos.astype(f32) >= low) & (key_pos <= query_pos)
        key_rows, value_rows = kbuf[j], vbuf[j]
        key_part = jnp.zeros((T, HD), f32)
        value_part = jnp.zeros((T, HD), f32)
        for h in range(HQ):
            cols = pl.ds(h * HD, HD)
            qh = q_all[:, :, cols].reshape(2 * T, HD)
            doh = do_all[:, :, cols].reshape(2 * T, HD)
            s = dot(key_rows, qh, ((1,), (1,)))
            prob = jnp.where(allowed, jnp.exp2(s * (SCALE * LOG2E) - row(HQ + h)), 0.0)
            dp = dot(value_rows, doh, ((1,), (1,)))
            ds = (prob * (dp - row(h)) * SCALE).astype(bf16)
            ds_buf[h, pl.ds(j * T, T), :] = ds
            key_part += dot(ds, qh, ((1,), (0,)))
            value_part += dot(prob.astype(bf16), doh, ((1,), (0,)))
        if j == 0:
            own_key, own_value = key_part, value_part
            wsum[:, pl.ds(0, HD)] = own_key
            wsum[:, pl.ds(HD, HD)] = own_value
        else:
            ret_send[j - 1, :, pl.ds(0, HD)] = key_part.astype(bf16)
            ret_send[j - 1, :, pl.ds(HD, HD)] = value_part.astype(bf16)
            send(
                ret_send.at[j - 1], ret_recv.at[j - 1], ret_s.at[j - 1], ret_r.at[j - 1], block_at(-2 * j)
            ).start()

    key_cat = kbuf[...].reshape(3 * T, HD)
    for h in range(HQ):
        part = dot(ds_buf[h], key_cat, ((0,), (0,)))
        dq_part[0, :, pl.ds(h * HD, HD)] = part[:T]
        dq_part[1, :, pl.ds(h * HD, HD)] = part[T:]
    cp_dq = send(dq_part.at[other], dq_recv, dq_s.at[0], dq_r.at[0], sib)
    cp_dq.start()

    x_own.wait()
    for copy in cp_x:
        copy.wait_recv()
    for yy in range(Y):
        xt[yy] = x_recv[yy].T

    rets = []
    for j in (1, 2):
        copy = send(ret_send.at[j - 1], ret_recv.at[j - 1], ret_s.at[j - 1], ret_r.at[j - 1], block_at(-2 * j))
        copy.wait_recv()
        rets.append(copy)
    mine = pl.ds(pl.multiple_of(c * T, T), T)
    theirs = pl.ds(pl.multiple_of(other * T, T), T)
    g_all[y, mine, :] = (wsum[...] + ret_recv[0].astype(f32) + ret_recv[1].astype(f32)).astype(bf16)
    cp_g = []
    for i, dy in enumerate((2, 1, 3)):
        copy = send(g_all.at[y, mine], g_all.at[y, mine], g_s.at[i], g_r.at[i], place(lax.rem(y + dy, Y), z, x, c))
        copy.start()
        cp_g.append(copy)
    cp_sib = send(g_all.at[y, mine], g_all.at[y, mine], g_s.at[3], g_r.at[3], sib)
    cp_sib.start()

    cp_dq.wait_recv()
    dq_ref[...] = (dq_part[c] + dq_recv[...]).astype(bf16)

    cp_sib.wait_recv()
    acc[...] = dot(xt[y], g_all[y], ((1,), (0,)))
    fwds = []
    for i, dy in ((1, 1), (2, 3), (0, 2)):
        from_y = lax.rem(y + Y - dy, Y)
        cp_g[i].wait_recv()
        fwd = send(g_all.at[from_y, mine], g_all.at[from_y, mine], fwd_s.at[i], fwd_s.at[3 + i], sib)
        fwd.start()
        fwds.append(fwd)
    for n, dy in enumerate((1, 3)):
        from_y = lax.rem(y + Y - dy, Y)
        fwds[n].wait_recv()
        acc[...] += dot(xt[from_y], g_all[from_y], ((1,), (0,)))
    last_y = lax.rem(y + 2, Y)
    fwds[2].wait_recv()
    part_rows = DC // 4
    slot = z * X + x
    for kz in range(4):
        rows = pl.ds(kz * part_rows, part_rows)
        acc[rows, :] += dot(xt[last_y, rows, :], g_all[last_y], ((1,), (0,)))
        for kx in range(X):
            for kc in range(C):
                at = kz * part_rows + kx * (C * ROWS) + kc * (C * ROWS - WIN)
                n = (kz * X + kx) * C + kc
                rs_send[n] = jnp.concatenate(
                    [acc[pl.ds(at, WIN), pl.ds(0, HD)], acc[pl.ds(at, WIN), pl.ds(HD, HD)]], axis=0
                ).astype(bf16)
        for kx in range(X):
            for kc in range(C):
                n = (kz * X + kx) * C + kc
                zz = c * (Z // C) + kz
                is_self = (zz == z) & (kx == x) & (kc == c)

                @pl.when(is_self)
                def _():
                    pltpu.make_async_copy(rs_send.at[n], rs_recv.at[slot], rs_r.at[0]).start()

                @pl.when(jnp.logical_not(is_self))
                def _():
                    send(rs_send.at[n], rs_recv.at[slot], rs_s.at[0], rs_r.at[0], place(y, zz, kx, kc)).start()

    send(rs_send, rs_recv, rs_s.at[0], rs_r.at[0], sib).wait_recv()
    total = rs_recv[0].astype(f32)
    for n in range(1, Z * X):
        total += rs_recv[n].astype(f32)
    wsum[pl.ds(0, 2 * WIN), pl.ds(0, HD)] = total
    low = jnp.concatenate([wsum[pl.ds(0, ROWS), pl.ds(0, HD)], wsum[pl.ds(WIN, ROWS), pl.ds(0, HD)]], axis=1)
    high = jnp.concatenate(
        [wsum[pl.ds(WIN - ROWS, ROWS), pl.ds(0, HD)], wsum[pl.ds(2 * WIN - ROWS, ROWS), pl.ds(0, HD)]], axis=1
    )
    rows_sum = jnp.where(c == 0, low, high)

    squares = jnp.sum(rows_sum * rows_sum, axis=0, keepdims=True)
    lane = squares[:, :HD] + squares[:, HD:]
    sq1[0] = jnp.broadcast_to(lane, (8, HD))

    def send_xy(i, _):
        to = place(lax.rem(y + i // X, Y), z, lax.rem(x + lax.rem(i, X), X), c)
        send(sq1.at[0], sq1.at[i], sq_s.at[0], sq_r.at[0], to).start()
        return 0

    lax.fori_loop(1, Y * X, send_xy, 0)
    send(sq1.at[pl.ds(1, Y * X - 1)], sq1.at[pl.ds(1, Y * X - 1)], sq_s.at[0], sq_r.at[0], sib).wait_recv()
    sq2[0] = jnp.sum(sq1[...], axis=0)

    def send_zc(i, _):
        to = place(y, lax.rem(z + i // C, Z), x, lax.rem(c + lax.rem(i, C), C))
        send(sq2.at[0], sq2.at[i], sq_s.at[1], sq_r.at[1], to).start()
        return 0

    lax.fori_loop(1, Z * C, send_zc, 0)
    send(sq2.at[pl.ds(1, Z * C - 1)], sq2.at[pl.ds(1, Z * C - 1)], sq_s.at[1], sq_r.at[1], sib).wait_recv()
    lanes = jnp.sum(sq2[...], axis=0)
    square_total = jnp.sum(lanes[0:1], axis=1, keepdims=True)
    limit = math.sqrt(D * 2 * HD)
    clip = jnp.minimum(1.0, limit / (jnp.sqrt(square_total) + 1e-6))
    w_ref[...] = rows_sum * clip

    for copy in [cp_q, cp_do, cp_st, *cp_kv, *cp_x, *rets, cp_dq, *cp_g, cp_sib, *fwds]:
        copy.wait_send()

    @pl.when(self_rs)
    def _():
        part = pl.ds(0, Z * X - 1)
        send(rs_send.at[part], rs_recv.at[part], rs_s.at[0], rs_r.at[0], sib).wait_send()

    @pl.when(jnp.logical_not(self_rs))
    def _():
        send(rs_send, rs_recv, rs_s.at[0], rs_r.at[0], sib).wait_send()

    send(sq1.at[pl.ds(1, Y * X - 1)], sq1.at[pl.ds(1, Y * X - 1)], sq_s.at[0], sq_r.at[0], sib).wait_send()
    send(sq2.at[pl.ds(1, Z * C - 1)], sq2.at[pl.ds(1, Z * C - 1)], sq_s.at[1], sq_r.at[1], sib).wait_send()


def on_device(queries, keys, values, attention_out, output_grad, log_norm, layer_input, doc_start, visible_blocks):
    hbm = pl.BlockSpec(memory_space=pl.ANY)
    vmem = pl.BlockSpec(memory_space=pltpu.VMEM)
    dma = pltpu.SemaphoreType.DMA
    return pl.pallas_call(
        kernel,
        out_shape=(jax.ShapeDtypeStruct((ROWS, 2 * HD), f32), jax.ShapeDtypeStruct((T, HQ * HD), bf16)),
        in_specs=[hbm, hbm, hbm, hbm, hbm, vmem, hbm, vmem, vmem],
        out_specs=(vmem, vmem),
        scratch_shapes=[
            pltpu.VMEM((C, T, HQ * HD), bf16),
            pltpu.VMEM((C, T, HQ * HD), bf16),
            pltpu.VMEM((T, HQ * HD), bf16),
            pltpu.VMEM((3, T, HD), bf16),
            pltpu.VMEM((3, T, HD), bf16),
            pltpu.VMEM((C, 16, T), f32),
            pltpu.VMEM((HQ, 3 * T, 2 * T), bf16),
            pltpu.VMEM((2, T, 2 * HD), bf16),
            pltpu.VMEM((2, T, 2 * HD), bf16),
            pltpu.VMEM((C, T, HQ * HD), f32),
            pltpu.VMEM((T, HQ * HD), f32),
            pltpu.VMEM((Y, C * T, DC), bf16),
            pltpu.VMEM((Y, DC, C * T), bf16),
            pltpu.VMEM((Y, C * T, 2 * HD), bf16),
            pltpu.VMEM((DC, 2 * HD), f32),
            pltpu.VMEM((Z * X, 2 * WIN, HD), bf16),
            pltpu.VMEM((Z * X, 2 * WIN, HD), bf16),
            pltpu.VMEM((T, 2 * HD), f32),
            pltpu.VMEM((Y * X, 8, HD), f32),
            pltpu.VMEM((Z * C, 8, HD), f32),
            dma((6,)),
            dma((3,)),
            dma((3,)),
            dma((4,)),
            dma((4,)),
            dma((2,)),
            dma((2,)),
            dma((7,)),
            dma((7,)),
            dma((4,)),
            dma((4,)),
            dma((6,)),
            dma((1,)),
            dma((1,)),
            dma((1,)),
            dma((1,)),
            dma((2,)),
            dma((2,)),
        ],
        compiler_params=pltpu.CompilerParams(
            collective_id=0, has_side_effects=True, vmem_limit_bytes=40 * 2**20
        ),
        name="clip_attention_backward",
    )(
        queries,
        keys,
        values,
        attention_out,
        output_grad,
        log_norm,
        layer_input,
        doc_start.reshape(1, T),
        visible_blocks,
    )


def solution(mesh):
    both = ("inner", "outer")
    return jax.shard_map(
        on_device,
        mesh=mesh,
        in_specs=(
            P(both, None),
            P(both, None),
            P(both, None),
            P(both, None),
            P(both, None),
            P(None, both),
            P(both, None),
            P(both),
            P(both, None),
        ),
        out_specs=(P(both, None), P(both, None)),
        check_vma=False,
    )
```

time: 444 us -> 69.4 us (0.16)
  waiting for transfers between devices: 282 us -> 0 us
  blocking collectives: 77.7 us -> 0 us
  Pallas kernels: 0 us -> 59.6 us
  starting transfers between devices: 43.1 us -> 0 us
  between operations: 18.4 us -> 0.66 us
  matrix products: 11.3 us -> 0 us
  other arithmetic: 5.07 us -> 0 us
    unnamed x2 -> x0, waiting for transfers between devices: 280 us -> none
    psum x1 -> x0, blocking collectives: 77.7 us -> none  [on_device(): lax.psum(jnp.sum(weight_sum * weight_sum), ('inner', 'outer'))]
    pallas_call x0 -> x1, Pallas kernels: none -> 59.6 us  [on_device(): pl.pallas_call(kernel, out_shape=(jax.ShapeDtypeStruct((ROWS, 2 * HD), f3...]
    ppermute x18 -> x0, starting transfers between devices: 43.1 us -> none  [the longest x10 22.1 us: passed_along_2(): lax.ppermute(value, axis, [(i, (i + by) % size) for i in range(size)])]
    dot_general x26 -> x0, matrix products: 11.3 us -> none  [the longest x1 3.2 us: on_device(): lax.dot_general(layer_input, all_grads, (((0,), (0,)), ((), ())), preferr...]
  transfers between devices with their start and end apart: 19 -> 0, of which waited for: 4 -> 0; matrix products, arithmetic and copies ran while one was open for 3% -> 0% of each run, Pallas kernels for 0% -> 0%
where the time goes in v1:
time: 69.4 us; the launch traced here: 69.1 us
  Pallas kernels  59.6 us (86%)
  local copies, waits for them, and re-layouts  8.84 us (13%)
    pallas_call x1, Pallas kernels, on_device(): pl.pallas_call(kernel, out_shape=(jax.ShapeDtypeStruct((ROWS, 2 * HD), f3...  59.6 us
    unnamed x20, local copies, waits for them, and re-layouts  8.84 us

profile of v1, /device:TPU:1, one launch (start us, length us, event | category | flops | bytes accessed | tf_op | source)
XLA Modules:
  0.0 69.1 jit_solution(16230270808439225369)
XLA Ops:
  0.6 0.0 copy-start
  0.6 1.3 %copy-done = bf16[128,5120]{1,0:T(8,128)(2,1)S(1)} copy-done((bf16[128,5120]{1,0:T(8,128)(2,1)S(1)}, bf16[128,5120]{1,0:T(8,128)(2,1)}, u32[]{:S(2)}) %copy-start) | copy-done | bytes 1310744
  2.0 0.0 copy-start.1
  2.0 0.9 %copy-done.1 = bf16[128,640]{1,0:T(8,128)(2,1)S(1)} copy-done((bf16[128,640]{1,0:T(8,128)(2,1)S(1)}, bf16[128,640]{1,0:T(8,128)(2,1)}, u32[]{:S(2)}) %copy-start.1) | copy-done | bytes 163864
  2.9 0.0 copy-start.2
  2.9 0.9 %copy-done.2 = bf16[128,640]{1,0:T(8,128)(2,1)S(1)} copy-done((bf16[128,640]{1,0:T(8,128)(2,1)S(1)}, bf16[128,640]{1,0:T(8,128)(2,1)}, u32[]{:S(2)}) %copy-start.2) | copy-done | bytes 163864
  3.8 0.0 copy-start.3
  3.8 0.9 %copy-done.3 = bf16[128,640]{1,0:T(8,128)(2,1)S(1)} copy-done((bf16[128,640]{1,0:T(8,128)(2,1)S(1)}, bf16[128,640]{1,0:T(8,128)(2,1)}, u32[]{:S(2)}) %copy-start.3) | copy-done | bytes 163864
  4.7 0.0 copy-start.4
  4.7 0.8 %copy-done.4 = bf16[128,128]{1,0:T(8,128)(2,1)S(1)} copy-done((bf16[128,128]{1,0:T(8,128)(2,1)S(1)}, bf16[128,128]{1,0:T(8,128)(2,1)}, u32[]{:S(2)}) %copy-start.4) | copy-done | bytes 32792
  5.5 0.0 copy-start.5
  5.5 0.8 %copy-done.5 = bf16[128,128]{1,0:T(8,128)(2,1)S(1)} copy-done((bf16[128,128]{1,0:T(8,128)(2,1)S(1)}, bf16[128,128]{1,0:T(8,128)(2,1)}, u32[]{:S(2)}) %copy-start.5) | copy-done | bytes 32792
  6.2 0.0 copy-start.6
  6.2 0.7 copy-done.6
  6.9 0.0 copy-start.7
  6.9 0.7 copy-done.7
  7.6 0.0 copy-start.8
  7.6 0.7 copy-done.8
  8.2 59.6 %clip_attention_backward.1 = (f32[20,256]{1,0:T(8,128)S(1)}, bf16[128,640]{1,0:T(8,128)(2,1)S(1)}) custom-call(bf16[128,640]{1,0:T(8,128)(2,1)S(1)} %copy-done.1, bf16[128,128]{1,0:T(8,128)(2,1)S(1)} %copy-done.4, bf16[128,128]{1,0:T(8,128)(2,1)S(1)} %copy-done.5, bf16[128,640]{1,0:T(8,128)(2,1)S(1)} %copy-done.2, bf16[128,640]{1,0:T(8,128)(2,1)S(1)} %copy-done.3, ...), custom_call_target="tpu_custom_call" | custom-call | tf_op jit(solution)/shard_map/clip_attention_backward/pallas_call | solution.py:378
  67.8 0.6 copy.13
  68.4 0.7 copy.14
Async XLA Ops:
  0.6 1.3 %copy-start = (bf16[128,5120]{1,0:T(8,128)(2,1)S(1)}, bf16[128,5120]{1,0:T(8,128)(2,1)}, u32[]{:S(2)}) copy-start(bf16[128,5120]{1,0:T(8,128)(2,1)} %x_hbm.1) | copy-start | bytes 3932164
  2.0 0.9 %copy-start.1 = (bf16[128,640]{1,0:T(8,128)(2,1)S(1)}, bf16[128,640]{1,0:T(8,128)(2,1)}, u32[]{:S(2)}) copy-start(bf16[128,640]{1,0:T(8,128)(2,1)} %q_hbm.1) | copy-start | bytes 491524
  2.9 0.9 %copy-start.2 = (bf16[128,640]{1,0:T(8,128)(2,1)S(1)}, bf16[128,640]{1,0:T(8,128)(2,1)}, u32[]{:S(2)}) copy-start(bf16[128,640]{1,0:T(8,128)(2,1)} %o_hbm.1) | copy-start | bytes 491524
  3.8 0.9 %copy-start.3 = (bf16[128,640]{1,0:T(8,128)(2,1)S(1)}, bf16[128,640]{1,0:T(8,128)(2,1)}, u32[]{:S(2)}) copy-start(bf16[128,640]{1,0:T(8,128)(2,1)} %do_hbm.1) | copy-start | bytes 491524
  4.7 0.8 %copy-start.4 = (bf16[128,128]{1,0:T(8,128)(2,1)S(1)}, bf16[128,128]{1,0:T(8,128)(2,1)}, u32[]{:S(2)}) copy-start(bf16[128,128]{1,0:T(8,128)(2,1)} %k_hbm.1) | copy-start | bytes 98308
  5.5 0.8 %copy-start.5 = (bf16[128,128]{1,0:T(8,128)(2,1)S(1)}, bf16[128,128]{1,0:T(8,128)(2,1)}, u32[]{:S(2)}) copy-start(bf16[128,128]{1,0:T(8,128)(2,1)} %v_hbm.1) | copy-start | bytes 98308
  6.2 0.7 copy-start.6
  6.9 0.7 copy-start.7
  7.6 0.7 copy-start.8

commit v2 on v1

v2 whole, which is shorter than its diff:
```python
import math

import jax
import jax.numpy as jnp
from jax import lax
from jax.experimental import pallas as pl
from jax.experimental.pallas import tpu as pltpu
from jax.sharding import PartitionSpec as P

D = 5120
HD = 128
HQ = 5
T = 128
Y, Z, X, C = 4, 8, 4, 2
N = Y * Z * X * C
DY = D // Y
DC = DY // C
ROWS = D // N
PAIR = C * ROWS
FAR = 1.0e9
MESH = pl.DeviceIdType.MESH
f32, bf16 = jnp.float32, jnp.bfloat16
SCALE = 1.0 / math.sqrt(HD)
LOG2E = math.log2(math.e)


def place(y, z, x, c):
    return {"inner": y, "outer": (z * X + x) * C + c}


def dot(a, b, dims):
    return lax.dot_general(a, b, (dims, ((), ())), preferred_element_type=f32)


def kernel(
    q_hbm,
    k_hbm,
    v_hbm,
    o_hbm,
    do_hbm,
    lse_hbm,
    x_hbm,
    start_hbm,
    vis_hbm,
    w_ref,
    dq_ref,
    lse_ref,
    start_ref,
    vis_ref,
    q_all,
    do_all,
    o_own,
    kbuf,
    vbuf,
    stat,
    ds_buf,
    ret_send,
    ret_recv,
    dq_part,
    dq_recv,
    x_recv,
    xt,
    g_all,
    acc,
    rs_send,
    rs_recv,
    own,
    wsum,
    sq1,
    sq2,
    load_sem,
    qx_s,
    qx_r,
    kv_s,
    kv_r,
    ret_s,
    ret_r,
    x_s,
    x_r,
    g_s,
    g_r,
    fwd_s,
    dq_s,
    dq_r,
    rs_s,
    rs_r,
    w_s,
    w_r,
    sq_s,
    sq_r,
):
    y = lax.axis_index("inner")
    outer = lax.axis_index("outer")
    z = outer // (X * C)
    x = (outer // C) % X
    c = outer % C
    other = 1 - c
    block = y * (Z * X * C) + outer
    sib = place(y, z, x, other)
    taker = z // (Z // C) == c
    one = jnp.where(taker, 1, 0)

    def block_at(step):
        b = lax.rem(block + (step + N), N)
        return {"inner": b // (Z * X * C), "outer": lax.rem(b, Z * X * C)}

    def send(src, dst, ssem, rsem, device):
        copy = pltpu.make_async_remote_copy(
            src_ref=src, dst_ref=dst, send_sem=ssem, recv_sem=rsem, device_id=device, device_id_type=MESH
        )
        return copy

    late = []
    loads = [
        pltpu.make_async_copy(do_hbm, do_all.at[c], load_sem.at[0]),
        pltpu.make_async_copy(o_hbm, o_own, load_sem.at[1]),
        pltpu.make_async_copy(q_hbm, q_all.at[c], load_sem.at[2]),
        pltpu.make_async_copy(k_hbm, kbuf.at[0], load_sem.at[3]),
        pltpu.make_async_copy(v_hbm, vbuf.at[0], load_sem.at[4]),
        pltpu.make_async_copy(lse_hbm, lse_ref, load_sem.at[6]),
        pltpu.make_async_copy(start_hbm, start_ref, load_sem.at[7]),
        pltpu.make_async_copy(vis_hbm, vis_ref, load_sem.at[8]),
    ]
    for load in loads:
        load.start()

    barrier = pltpu.get_barrier_semaphore()

    def greet(device):
        pl.semaphore_signal(barrier, inc=1, device_id=device, device_id_type=MESH)

    def greet_zx(i, _):
        zz, xx = lax.rem(z + (Z // 2) + i // X, Z), lax.rem(x + 2 + lax.rem(i, X), X)

        @pl.when((zz != z) | (xx != x))
        def _():
            greet(place(y, zz, xx, c))

        return 0

    def greet_xy(i, _):
        greet(place(lax.rem(y + i // X, Y), z, lax.rem(x + lax.rem(i, X), X), c))
        return 0

    def greet_z(zz, _):
        cc = zz // (Z // C)

        @pl.when((zz != z) | (cc != c))
        def _():
            greet(place(y, zz, x, cc))

        return 0

    @pl.when(taker)
    def _():
        lax.fori_loop(0, Z * X, greet_zx, 0)

    lax.fori_loop(0, Z, greet_z, 0)

    @pl.when(taker)
    def _():
        lax.fori_loop(1, Y * X, greet_xy, 0)

    for step in (-4, 4, -2, 2):
        greet(block_at(step))
    for dy in (2, 1, 3):
        for cc in range(C):
            greet(place(lax.rem(y + dy, Y), z, x, cc))
    greet(sib)

    for i in (0, 1, 5, 6, 7):
        loads[i].wait()
    for h in range(HQ):
        cols = pl.ds(h * HD, HD)
        prod = do_all[c, :, cols].astype(f32) * o_own[:, cols].astype(f32)
        stat[c, pl.ds(h, 1), :] = jnp.sum(prod.T, axis=0, keepdims=True)
    stat[c, pl.ds(HQ, HQ), :] = lse_ref[...] * LOG2E
    first = start_ref[...].astype(f32)
    for d in range(5):
        kb = block - d
        wanted = jnp.where(kb >= 0, kb, -7)
        hit = jnp.max(jnp.where(vis_ref[...] == wanted, 1.0, 0.0), axis=1, keepdims=True)
        stat[c, pl.ds(10 + d, 1), :] = jnp.where(hit > 0.5, first, FAR)
    stat[c, pl.ds(15, 1), :] = jnp.full((1, T), FAR, f32)

    always = 1 + 4 + 2 * (Y - 1) + Z // C * X
    pl.semaphore_wait(barrier, always + one * (Y * X - 1 + Z * C - 1 - 1))

    cp_q = send(q_hbm, q_all.at[c], qx_s.at[0], qx_r.at[0], sib)
    cp_do = send(do_hbm, do_all.at[c], qx_s.at[1], qx_r.at[1], sib)
    cp_st = send(stat.at[c], stat.at[c], qx_s.at[2], qx_r.at[2], sib)
    cp_kv = []
    for j in (1, 2):
        cp_kv.append(send(k_hbm, kbuf.at[j], kv_s.at[2 * j - 2], kv_r.at[2 * j - 2], block_at(2 * j)))
        cp_kv.append(send(v_hbm, vbuf.at[j], kv_s.at[2 * j - 1], kv_r.at[2 * j - 1], block_at(2 * j)))
    for copy in cp_kv:
        copy.start()
    cp_st.start()
    cp_q.start()
    cp_do.start()

    def x_cols(yy, cc):
        return x_hbm.at[:, pl.ds(pl.multiple_of(yy * DY + cc * DC, HD), DC)]

    x_own = pltpu.make_async_copy(x_cols(y, c), x_recv.at[y, pl.ds(pl.multiple_of(c * T, T), T)], load_sem.at[5])
    x_own.start()
    my_rows = x_recv.at[y, pl.ds(pl.multiple_of(c * T, T), T)]
    cp_x = []
    for i, (dy, dc) in enumerate([(0, 1), (1, 0), (3, 0), (1, 1), (3, 1), (2, 0), (2, 1)]):
        yy, cc = lax.rem(y + dy, Y), lax.rem(c + dc, C)
        copy = send(x_cols(yy, cc), my_rows, x_s.at[i], x_r.at[i], place(yy, z, x, cc))
        copy.start()
        cp_x.append(copy)

    for load in loads[2:5]:
        load.wait()
    cp_q.wait_recv()
    cp_do.wait_recv()
    cp_st.wait_recv()

    def row(r):
        return jnp.concatenate([stat[0, pl.ds(r, 1), :], stat[1, pl.ds(r, 1), :]], axis=1)

    iota_u = lax.broadcasted_iota(jnp.int32, (T, 2 * T), 0)
    iota_t = lax.broadcasted_iota(jnp.int32, (T, 2 * T), 1)
    pair_first = (block - c) * T
    query_pos = pair_first + iota_t
    cp_ret = []
    for j in range(3):
        if j > 0:
            cp_kv[2 * j - 2].wait_recv()
            cp_kv[2 * j - 1].wait_recv()
        key_pos = (block - 2 * j) * T + iota_u
        lows = []
        for i in range(C):
            d0, d1 = i + 2 * j, i - 1 + 2 * j
            at0, at1 = 10 + min(d0, 5), 10 + (d1 if d1 >= 0 else 5)
            lows.append(jnp.where(c == 0, stat[i, pl.ds(at0, 1), :], stat[i, pl.ds(at1, 1), :]))
        low = jnp.concatenate(lows, axis=1)
        allowed = (key_pos.astype(f32) >= low) & (key_pos <= query_pos)
        key_rows, value_rows = kbuf[j], vbuf[j]
        key_part = jnp.zeros((T, HD), f32)
        value_part = jnp.zeros((T, HD), f32)
        for h in range(HQ):
            cols = pl.ds(h * HD, HD)
            qh = q_all[:, :, cols].reshape(2 * T, HD)
            doh = do_all[:, :, cols].reshape(2 * T, HD)
            s = dot(key_rows, qh, ((1,), (1,)))
            prob = jnp.where(allowed, jnp.exp2(s * (SCALE * LOG2E) - row(HQ + h)), 0.0)
            dp = dot(value_rows, doh, ((1,), (1,)))
            ds = (prob * (dp - row(h)) * SCALE).astype(bf16)
            ds_buf[h, pl.ds(j * T, T), :] = ds
            key_part += dot(ds, qh, ((1,), (0,)))
            value_part += dot(prob.astype(bf16), doh, ((1,), (0,)))
        if j == 0:
            own[:, pl.ds(0, HD)] = key_part
            own[:, pl.ds(HD, HD)] = value_part
        else:
            ret_send[j - 1, :, pl.ds(0, HD)] = key_part.astype(bf16)
            ret_send[j - 1, :, pl.ds(HD, HD)] = value_part.astype(bf16)
            copy = send(ret_send.at[j - 1], ret_recv.at[j - 1], ret_s.at[j - 1], ret_r.at[j - 1], block_at(-2 * j))
            copy.start()
            cp_ret.append(copy)

    key_cat = kbuf[...].reshape(3 * T, HD)
    for h in range(HQ):
        part = dot(ds_buf[h], key_cat, ((0,), (0,)))
        dq_part[0, :, pl.ds(h * HD, HD)] = part[:T]
        dq_part[1, :, pl.ds(h * HD, HD)] = part[T:]
    cp_dq = send(dq_part.at[other], dq_recv, dq_s.at[0], dq_r.at[0], sib)
    cp_dq.start()

    for copy in cp_ret:
        copy.wait_recv()
    mine = pl.ds(pl.multiple_of(c * T, T), T)
    g_all[y, mine, :] = (own[...] + ret_recv[0].astype(f32) + ret_recv[1].astype(f32)).astype(bf16)
    cp_g = []
    for i, dy in enumerate((2, 1, 3)):
        copy = send(g_all.at[y, mine], g_all.at[y, mine], g_s.at[i], g_r.at[i], place(lax.rem(y + dy, Y), z, x, c))
        copy.start()
        cp_g.append(copy)
    cp_sib = send(g_all.at[y, mine], g_all.at[y, mine], g_s.at[3], g_r.at[3], sib)
    cp_sib.start()

    cp_dq.wait_recv()
    dq_ref[...] = (dq_part[c] + dq_recv[...]).astype(bf16)

    def from_y(dy):
        return lax.rem(y + Y - dy, Y)

    def pass_on(i, dy):
        cp_g[i].wait_recv()
        part = g_all.at[from_y(dy), mine]
        fwd = send(part, part, fwd_s.at[i], fwd_s.at[3 + i], sib)
        fwd.start()
        return fwd

    x_own.wait()
    cp_x[0].wait_recv()
    xt[y] = x_recv[y].T
    for copy in cp_x[1:5]:
        copy.wait_recv()
    for dy in (1, 3):
        xt[from_y(dy)] = x_recv[from_y(dy)].T
    fwds = [pass_on(1, 1), pass_on(2, 3)]
    for copy in cp_x[5:]:
        copy.wait_recv()
    xt[from_y(2)] = x_recv[from_y(2)].T
    cp_sib.wait_recv()
    acc[...] = dot(xt[y], g_all[y], ((1,), (0,)))
    fwds.append(pass_on(0, 2))
    for n, dy in enumerate((1, 3)):
        fwds[n].wait_recv()
        acc[...] += dot(xt[from_y(dy)], g_all[from_y(dy)], ((1,), (0,)))
    last_y = from_y(2)
    fwds[2].wait_recv()
    part_rows = PAIR * X
    slot = z * X + x
    for kz in range(Z // C):
        zz = c * (Z // C) + kz
        rows = pl.ds(kz * part_rows, part_rows)
        acc[rows, :] += dot(xt[last_y, rows, :], g_all[last_y], ((1,), (0,)))
        for kx in range(X):
            n = kz * X + kx
            at = pl.ds(n * PAIR, PAIR)
            rs_send[n] = jnp.concatenate([acc[at, pl.ds(0, HD)], acc[at, pl.ds(HD, HD)]], axis=0).astype(bf16)
        for kx in range(X):
            n = kz * X + kx
            is_self = (zz == z) & (kx == x)

            @pl.when(is_self)
            def _():
                pltpu.make_async_copy(rs_send.at[n], rs_recv.at[slot], rs_r.at[0]).start()

            @pl.when(jnp.logical_not(is_self))
            def _():
                send(rs_send.at[n], rs_recv.at[slot], rs_s.at[0], rs_r.at[0], place(y, zz, kx, c)).start()

    def rs_left():
        whole = Z // C * X

        @pl.when(taker)
        def _():
            part = pl.ds(0, whole - 1)
            send(rs_send.at[part], rs_recv.at[part], rs_s.at[0], rs_r.at[0], sib).wait_send()

        @pl.when(jnp.logical_not(taker))
        def _():
            part = pl.ds(0, whole)
            send(rs_send.at[part], rs_recv.at[part], rs_s.at[0], rs_r.at[0], sib).wait_send()

    late.append(rs_left)
    cp_w = send(wsum, wsum, w_s.at[0], w_r.at[0], sib)
    some_xy = pl.ds(1, Y * X - 1)
    all_xy = send(sq1.at[some_xy], sq1.at[some_xy], sq_s.at[0], sq_r.at[0], sib)
    some_zc = send(sq2.at[pl.ds(0, Z - 1)], sq2.at[pl.ds(0, Z - 1)], sq_s.at[1], sq_r.at[1], sib)
    all_zc = send(sq2, sq2, sq_s.at[1], sq_r.at[1], sib)

    def send_xy(i, _):
        to = place(lax.rem(y + i // X, Y), z, lax.rem(x + lax.rem(i, X), X), c)
        send(sq1.at[0], sq1.at[i], sq_s.at[0], sq_r.at[0], to).start()
        return 0

    def send_zc(i, _):
        to = place(y, lax.rem(z + Z // 2 + i // C, Z), x, lax.rem(c + 1 + lax.rem(i, C), C))

        @pl.when(i != Z + 1)
        def _():
            send(sq2.at[z], sq2.at[z], sq_s.at[1], sq_r.at[1], to).start()

        return 0

    @pl.when(taker)
    def _():
        send(rs_send, rs_recv, rs_s.at[0], rs_r.at[0], sib).wait_recv()
        total = rs_recv[0].astype(f32)
        for n in range(1, Z * X):
            total += rs_recv[n].astype(f32)
        wsum[...] = total
        cp_w.start()
        sq1[0] = jnp.broadcast_to(jnp.sum(total * total, axis=0, keepdims=True), (8, HD))
        lax.fori_loop(1, Y * X, send_xy, 0)
        all_xy.wait_recv()
        sq2[z] = jnp.sum(sq1[...], axis=0)
        lax.fori_loop(0, Z * C, send_zc, 0)
        some_zc.wait_recv()

    @pl.when(jnp.logical_not(taker))
    def _():
        cp_w.wait_recv()
        all_zc.wait_recv()

    def sums_left():
        @pl.when(taker)
        def _():
            cp_w.wait_send()
            all_xy.wait_send()
            for part in (pl.ds(0, Z), pl.ds(0, Z - 1)):
                send(sq2.at[part], sq2.at[part], sq_s.at[1], sq_r.at[1], sib).wait_send()

    late.append(sums_left)
    parts = []
    for k in range(C):
        at, then = pl.ds(k * ROWS, ROWS), pl.ds(PAIR + k * ROWS, ROWS)
        parts.append(jnp.concatenate([wsum[at, :], wsum[then, :]], axis=1))
    rows_sum = jnp.where(c == 0, parts[0], parts[1])

    lanes = jnp.sum(sq2[...], axis=0)
    square_total = jnp.sum(lanes[0:1], axis=1, keepdims=True)
    limit = math.sqrt(D * 2 * HD)
    clip = jnp.minimum(1.0, limit / (jnp.sqrt(square_total) + 1e-6))
    w_ref[...] = rows_sum * clip

    for copy in [cp_q, cp_do, cp_st, *cp_kv, *cp_x, *cp_ret, cp_dq, *cp_g, cp_sib, *fwds]:
        copy.wait_send()

    for wait in late:
        wait()


def on_device(queries, keys, values, attention_out, output_grad, log_norm, layer_input, doc_start, visible_blocks):
    hbm = pl.BlockSpec(memory_space=pl.ANY)
    dma = pltpu.SemaphoreType.DMA
    return pl.pallas_call(
        kernel,
        out_shape=(pltpu.VMEM((ROWS, 2 * HD), f32), pltpu.VMEM((T, HQ * HD), bf16)),
        in_specs=[hbm] * 9,
        out_specs=(pl.BlockSpec(memory_space=pltpu.VMEM),) * 2,
        scratch_shapes=[
            pltpu.VMEM((HQ, T), f32),
            pltpu.VMEM((1, T), jnp.int32),
            pltpu.VMEM((1, 5), jnp.int32),
            pltpu.VMEM((C, T, HQ * HD), bf16),
            pltpu.VMEM((C, T, HQ * HD), bf16),
            pltpu.VMEM((T, HQ * HD), bf16),
            pltpu.VMEM((3, T, HD), bf16),
            pltpu.VMEM((3, T, HD), bf16),
            pltpu.VMEM((C, 16, T), f32),
            pltpu.VMEM((HQ, 3 * T, 2 * T), bf16),
            pltpu.VMEM((2, T, 2 * HD), bf16),
            pltpu.VMEM((2, T, 2 * HD), bf16),
            pltpu.VMEM((C, T, HQ * HD), f32),
            pltpu.VMEM((T, HQ * HD), f32),
            pltpu.VMEM((Y, C * T, DC), bf16),
            pltpu.VMEM((Y, DC, C * T), bf16),
            pltpu.VMEM((Y, C * T, 2 * HD), bf16),
            pltpu.VMEM((DC, 2 * HD), f32),
            pltpu.VMEM((Z * X, 2 * PAIR, HD), bf16),
            pltpu.VMEM((Z * X, 2 * PAIR, HD), bf16),
            pltpu.VMEM((T, 2 * HD), f32),
            pltpu.VMEM((2 * PAIR, HD), f32),
            pltpu.VMEM((Y * X, 8, HD), f32),
            pltpu.VMEM((Z, 8, HD), f32),
            dma((9,)),
            dma((3,)),
            dma((3,)),
            dma((4,)),
            dma((4,)),
            dma((2,)),
            dma((2,)),
            dma((7,)),
            dma((7,)),
            dma((4,)),
            dma((4,)),
            dma((6,)),
            dma((1,)),
            dma((1,)),
            dma((1,)),
            dma((1,)),
            dma((1,)),
            dma((1,)),
            dma((2,)),
            dma((2,)),
        ],
        compiler_params=pltpu.CompilerParams(
            collective_id=0, has_side_effects=True, vmem_limit_bytes=56 * 2**20
        ),
        name="clip_attention_backward",
    )(
        queries,
        keys,
        values,
        attention_out,
        output_grad,
        log_norm,
        layer_input,
        doc_start.reshape(1, T),
        visible_blocks,
    )


def solution(mesh):
    both = ("inner", "outer")
    return jax.shard_map(
        on_device,
        mesh=mesh,
        in_specs=(
            P(both, None),
            P(both, None),
            P(both, None),
            P(both, None),
            P(both, None),
            P(None, both),
            P(both, None),
            P(both),
            P(both, None),
        ),
        out_specs=(P(both, None), P(both, None)),
        check_vma=False,
    )
```

time: 69.4 us -> 57.7 us (0.83)
  local copies, waits for them, and re-layouts: 8.84 us -> 1.28 us
  Pallas kernels: 59.6 us -> 55.7 us
    unnamed x20 -> x2, local copies, waits for them, and re-layouts: 8.84 us -> 1.28 us
    pallas_call x1, Pallas kernels: 59.6 us -> 55.7 us  [on_device(): pl.pallas_call(kernel, out_shape=(pltpu.VMEM((ROWS, 2 * HD), f32), pltpu....]
where the time goes in v2:
time: 57.7 us; the launch traced here: 57.6 us
  Pallas kernels  55.7 us (97%)
  local copies, waits for them, and re-layouts  1.28 us (2%)
  between operations  0.64 us (1%)
    pallas_call x1, Pallas kernels, on_device(): pl.pallas_call(kernel, out_shape=(pltpu.VMEM((ROWS, 2 * HD), f32), pltpu....  55.7 us
    unnamed x2, local copies, waits for them, and re-layouts  1.28 us

profile of v2, /device:TPU:1, one launch (start us, length us, event | category | flops | bytes accessed | tf_op | source)
XLA Modules:
  0.0 57.6 jit_solution(13155894181241447952)
XLA Ops:
  0.6 55.7 %clip_attention_backward.1 = (f32[20,256]{1,0:T(8,128)S(1)}, bf16[128,640]{1,0:T(8,128)(2,1)S(1)}) custom-call(bf16[128,640]{1,0:T(8,128)(2,1)} %q_hbm.1, bf16[128,128]{1,0:T(8,128)(2,1)} %k_hbm.1, bf16[128,128]{1,0:T(8,128)(2,1)} %v_hbm.1, bf16[128,640]{1,0:T(8,128)(2,1)} %o_hbm.1, bf16[128,640]{1,0:T(8,128)(2,1)} %do_hbm.1, f32[5,128]{1,0:T(8,128)} %lse_hbm.1, ...), custom_call_target="tpu_custom_call" | custom-call | tf_op jit(solution)/shard_map/clip_attention_backward/pallas_call | solution.py:424
  56.3 0.6 %copy.13 = f32[20,256]{1,0:T(8,128)} copy(f32[20,256]{1,0:T(8,128)S(1)} %get-tuple-element.2) | data formatting | bytes 40960
  56.9 0.7 %copy.14 = bf16[128,640]{1,0:T(8,128)(2,1)} copy(bf16[128,640]{1,0:T(8,128)(2,1)S(1)} %get-tuple-element.3) | data formatting | bytes 327680

commit v3 on v2

v3 whole, which is shorter than its diff:
```python
import math

import jax
import jax.numpy as jnp
from jax import lax
from jax.experimental import pallas as pl
from jax.experimental.pallas import tpu as pltpu
from jax.sharding import PartitionSpec as P

D = 5120
HD = 128
HQ = 5
T = 128
Y, Z, X, C = 4, 8, 4, 2
N = Y * Z * X * C
GROUP = 4
UNIT = D // GROUP
HALF = UNIT // C
ROWS = D // N
PAIR = C * ROWS
MSG = 48
FAR = 1.0e9
MESH = pl.DeviceIdType.MESH
f32, bf16 = jnp.float32, jnp.bfloat16
SCALE = 1.0 / math.sqrt(HD)
LOG2E = math.log2(math.e)


def place(y, z, x, c):
    return {"inner": y, "outer": (z * X + x) * C + c}


def dot(a, b, dims):
    return lax.dot_general(a, b, (dims, ((), ())), preferred_element_type=f32)


def kernel(
    q_hbm,
    k_hbm,
    v_hbm,
    o_hbm,
    do_hbm,
    lse_hbm,
    x_hbm,
    start_hbm,
    vis_hbm,
    w_ref,
    dq_ref,
    lse_ref,
    start_ref,
    vis_ref,
    q_all,
    do_all,
    o_own,
    kbuf,
    vbuf,
    stat,
    p_buf,
    ds_buf,
    ret_send,
    ret_recv,
    dq_part,
    dq_recv,
    x_recv,
    xt,
    own,
    g_all,
    acc,
    ex_send,
    ex_recv,
    rs_send,
    rs_recv,
    wsum,
    sq1,
    sq2,
    load_sem,
    qx_s,
    qx_r,
    kv_s,
    kv_r,
    ret_s,
    ret_r,
    x_s,
    x_r,
    g_s,
    g_r,
    dq_s,
    dq_r,
    ex_s,
    ex_r,
    rs_s,
    rs_r,
    w_s,
    w_r,
    sq_s,
    sq_r,
):
    y = lax.axis_index("inner")
    outer = lax.axis_index("outer")
    z = outer // (X * C)
    x = (outer // C) % X
    c = outer % C
    other = 1 - c
    block = y * (Z * X * C) + outer
    sib = place(y, z, x, other)
    taker = z // (Z // C) == c
    one = jnp.where(taker, 1, 0)
    ay, az = lax.rem(y, 2), lax.rem(z, 2)
    pair_y = lax.rem(y + jnp.where(ay == c, 1, Y - 1), Y)
    pair_z = lax.rem(z + jnp.where(az == c, 1, Z - 1), Z)
    peers = [(pair_y, z), (y, pair_z), (pair_y, pair_z)]

    def member(yy, zz):
        return 2 * lax.rem(yy, 2) + lax.rem(zz, 2)

    def unit_owner(yy, zz):
        return 1 - lax.rem(yy, 2) + 2 * lax.rem(zz, 2)

    me = member(y, z)

    def block_at(step):
        b = lax.rem(block + (step + N), N)
        return {"inner": b // (Z * X * C), "outer": lax.rem(b, Z * X * C)}

    def send(src, dst, ssem, rsem, device):
        copy = pltpu.make_async_remote_copy(
            src_ref=src, dst_ref=dst, send_sem=ssem, recv_sem=rsem, device_id=device, device_id_type=MESH
        )
        return copy

    late = []
    loads = [
        pltpu.make_async_copy(do_hbm, do_all.at[c], load_sem.at[0]),
        pltpu.make_async_copy(o_hbm, o_own, load_sem.at[1]),
        pltpu.make_async_copy(q_hbm, q_all.at[c], load_sem.at[2]),
        pltpu.make_async_copy(k_hbm, kbuf.at[0], load_sem.at[3]),
        pltpu.make_async_copy(v_hbm, vbuf.at[0], load_sem.at[4]),
        pltpu.make_async_copy(lse_hbm, lse_ref, load_sem.at[6]),
        pltpu.make_async_copy(start_hbm, start_ref, load_sem.at[7]),
        pltpu.make_async_copy(vis_hbm, vis_ref, load_sem.at[8]),
    ]
    for load in loads:
        load.start()

    barrier = pltpu.get_barrier_semaphore()

    def greet(device):
        pl.semaphore_signal(barrier, inc=1, device_id=device, device_id_type=MESH)

    def greet_sources(i, _):
        yy = 1 - ay + 2 * (i // (Z // 2 * X))
        zz = y // 2 + 2 * lax.rem(i // X, Z // 2)
        greet(place(yy, zz, lax.rem(i, X), c))
        return 0

    def greet_xy(i, _):
        greet(place(lax.rem(y + i // X, Y), z, lax.rem(x + lax.rem(i, X), X), c))
        return 0

    def greet_z(zz, _):
        cc = zz // (Z // C)

        @pl.when((zz != z) | (cc != c))
        def _():
            greet(place(y, zz, x, cc))

        return 0

    @pl.when(taker)
    def _():
        lax.fori_loop(0, Z * X, greet_sources, 0)

    lax.fori_loop(0, Z, greet_z, 0)

    @pl.when(taker)
    def _():
        lax.fori_loop(1, Y * X, greet_xy, 0)

    for step in (-4, 4, -2, 2):
        greet(block_at(step))
    for yy, zz in peers:
        greet(place(yy, zz, x, c))
    greet(sib)

    for i in (0, 1, 5, 6, 7):
        loads[i].wait()
    for h in range(HQ):
        cols = pl.ds(h * HD, HD)
        prod = do_all[c, :, cols].astype(f32) * o_own[:, cols].astype(f32)
        stat[c, pl.ds(h, 1), :] = jnp.sum(prod.T, axis=0, keepdims=True)
    stat[c, pl.ds(HQ, HQ), :] = lse_ref[...] * LOG2E
    first = start_ref[...].astype(f32)
    for d in range(5):
        kb = block - d
        wanted = jnp.where(kb >= 0, kb, -7)
        hit = jnp.max(jnp.where(vis_ref[...] == wanted, 1.0, 0.0), axis=1, keepdims=True)
        stat[c, pl.ds(10 + d, 1), :] = jnp.where(hit > 0.5, first, FAR)
    stat[c, pl.ds(15, 1), :] = jnp.full((1, T), FAR, f32)

    always = 1 + 4 + 3 + Z // C * X
    pl.semaphore_wait(barrier, always + one * (Y * X - 1 + Z * C - 1))

    cp_q = send(q_hbm, q_all.at[c], qx_s.at[0], qx_r.at[0], sib)
    cp_do = send(do_hbm, do_all.at[c], qx_s.at[1], qx_r.at[1], sib)
    cp_st = send(stat.at[c], stat.at[c], qx_s.at[2], qx_r.at[2], sib)
    cp_k, cp_v = [
        [send(src, buf.at[j], kv_s.at[2 * n + j - 1], kv_r.at[2 * n + j - 1], block_at(2 * j)) for j in (1, 2)]
        for n, (src, buf) in enumerate(((k_hbm, kbuf), (v_hbm, vbuf)))
    ]
    for copy in [*cp_k, cp_st, cp_q, cp_do, *cp_v]:
        copy.start()

    def x_cols(yy, zz):
        return x_hbm.at[:, pl.ds(pl.multiple_of(unit_owner(yy, zz) * UNIT, HD), UNIT)]

    x_own = pltpu.make_async_copy(x_cols(y, z), x_recv.at[me], load_sem.at[5])
    x_own.start()
    cp_x = []
    for i, (yy, zz) in enumerate(peers):
        copy = send(x_cols(yy, zz), x_recv.at[me], x_s.at[i], x_r.at[i], place(yy, zz, x, c))
        copy.start()
        cp_x.append(copy)

    for load in loads[2:5]:
        load.wait()
    cp_q.wait_recv()
    cp_do.wait_recv()
    cp_st.wait_recv()

    def row(r):
        return jnp.concatenate([stat[0, pl.ds(r, 1), :], stat[1, pl.ds(r, 1), :]], axis=1)

    iota_u = lax.broadcasted_iota(jnp.int32, (T, 2 * T), 0)
    iota_t = lax.broadcasted_iota(jnp.int32, (T, 2 * T), 1)
    pair_first = (block - c) * T
    query_pos = pair_first + iota_t

    def probs(j):
        key_pos = (block - 2 * j) * T + iota_u
        lows = []
        for i in range(C):
            d0, d1 = i + 2 * j, i - 1 + 2 * j
            at0, at1 = 10 + min(d0, 5), 10 + (d1 if d1 >= 0 else 5)
            lows.append(jnp.where(c == 0, stat[i, pl.ds(at0, 1), :], stat[i, pl.ds(at1, 1), :]))
        low = jnp.concatenate(lows, axis=1)
        allowed = (key_pos.astype(f32) >= low) & (key_pos <= query_pos)
        key_rows = kbuf[j]
        part = jnp.zeros((T, HD), f32)
        for h in range(HQ):
            cols = pl.ds(h * HD, HD)
            s = dot(key_rows, q_all[:, :, cols].reshape(2 * T, HD), ((1,), (1,)))
            prob = jnp.where(allowed, jnp.exp2(s * (SCALE * LOG2E) - row(HQ + h)), 0.0)
            p_buf[j, h] = prob
            part += dot(prob.astype(bf16), do_all[:, :, cols].reshape(2 * T, HD), ((1,), (0,)))
        return part

    def score_grads(j):
        value_rows = vbuf[j]
        part = jnp.zeros((T, HD), f32)
        for h in range(HQ):
            cols = pl.ds(h * HD, HD)
            dp = dot(value_rows, do_all[:, :, cols].reshape(2 * T, HD), ((1,), (1,)))
            ds = (p_buf[j, h] * (dp - row(h)) * SCALE).astype(bf16)
            ds_buf[h, pl.ds(j * T, T), :] = ds
            part += dot(ds, q_all[:, :, cols].reshape(2 * T, HD), ((1,), (0,)))
        return part

    def give_back(n, j, part):
        k = 2 * n + j - 1
        ret_send[k] = part.astype(bf16)
        copy = send(ret_send.at[k], ret_recv.at[k], ret_s.at[k], ret_r.at[k], block_at(-2 * j))
        copy.start()
        return copy

    cp_ret = []
    own[0] = probs(0)
    own[1] = score_grads(0)
    for j in (1, 2):
        cp_k[j - 1].wait_recv()
        cp_ret.append(give_back(0, j, probs(j)))
    for j in (1, 2):
        cp_v[j - 1].wait_recv()
        cp_ret.append(give_back(1, j, score_grads(j)))

    key_cat = kbuf[...].reshape(3 * T, HD)
    for h in range(HQ):
        part = dot(ds_buf[h], key_cat, ((0,), (0,)))
        dq_part[0, :, pl.ds(h * HD, HD)] = part[:T]
        dq_part[1, :, pl.ds(h * HD, HD)] = part[T:]
    cp_dq = send(dq_part.at[other], dq_recv, dq_s.at[0], dq_r.at[0], sib)
    cp_dq.start()

    x_own.wait()
    for copy in cp_x:
        copy.wait_recv()
    for m in range(GROUP):
        for hc in range(C):
            xt[hc, :, pl.ds(m * T, T)] = x_recv[m, :, pl.ds(hc * HALF, HALF)].T

    cp_g = []
    for n in range(2):
        cp_ret[2 * n].wait_recv()
        cp_ret[2 * n + 1].wait_recv()
        g_all[n, me] = (own[n] + ret_recv[2 * n].astype(f32) + ret_recv[2 * n + 1].astype(f32)).astype(bf16)
        mine = g_all.at[n, me]
        for i, (yy, zz) in reversed(list(enumerate(peers))):
            copy = send(mine, mine, g_s.at[n, i], g_r.at[n, i], place(yy, zz, x, c))
            copy.start()
            cp_g.append(copy)

    cp_dq.wait_recv()
    dq_ref[...] = (dq_part[c] + dq_recv[...]).astype(bf16)

    slot = (y // 2 * (Z // 2) + z // 2) * X + x
    to_y = unit_owner(y, z)
    part_rows = PAIR * X
    cp_ex = []
    for n in range(2):
        for copy in cp_g[3 * n : 3 * n + 3]:
            copy.wait_recv()
        grads = g_all[n].reshape(GROUP * T, HD)
        ex_send[n] = dot(xt[other], grads, ((1,), (0,))).astype(bf16)
        copy = send(ex_send.at[n], ex_recv.at[n], ex_s.at[n], ex_r.at[n], sib)
        copy.start()
        cp_ex.append(copy)
        acc[...] = dot(xt[c], grads, ((1,), (0,)))
        copy.wait_recv()
        for kz in range(Z // C):
            rows = pl.ds(kz * part_rows, part_rows)
            acc[rows, :] += ex_recv[n, rows, :].astype(f32)
            for kx in range(X):
                m = kz * X + kx
                part = jnp.concatenate([acc[pl.ds(m * PAIR, PAIR), :], jnp.zeros((MSG - PAIR, HD), f32)], axis=0)
                rs_send[n, m] = part.astype(bf16)
                send(
                    rs_send.at[n, m],
                    rs_recv.at[n, slot],
                    rs_s.at[n],
                    rs_r.at[n],
                    place(to_y, c * (Z // C) + kz, kx, c),
                ).start()

    def rs_left():
        for n in range(2):
            whole = rs_recv.at[n, pl.ds(0, Z // C * X)]
            send(rs_send.at[n], whole, rs_s.at[n], rs_r.at[n], sib).wait_send()

    late.append(rs_left)
    cp_w = send(wsum, wsum, w_s.at[0], w_r.at[0], sib)
    some_xy = pl.ds(1, Y * X - 1)
    all_xy = send(sq1.at[some_xy], sq1.at[some_xy], sq_s.at[0], sq_r.at[0], sib)
    some_zc = send(sq2.at[pl.ds(0, Z - 1)], sq2.at[pl.ds(0, Z - 1)], sq_s.at[1], sq_r.at[1], sib)
    all_zc = send(sq2, sq2, sq_s.at[1], sq_r.at[1], sib)

    def send_xy(i, _):
        to = place(lax.rem(y + i // X, Y), z, lax.rem(x + lax.rem(i, X), X), c)
        send(sq1.at[0], sq1.at[i], sq_s.at[0], sq_r.at[0], to).start()
        return 0

    def send_zc(i, _):
        to = place(y, lax.rem(z + Z // 2 + i // C, Z), x, lax.rem(c + 1 + lax.rem(i, C), C))

        @pl.when(i != Z + 1)
        def _():
            send(sq2.at[z], sq2.at[z], sq_s.at[1], sq_r.at[1], to).start()

        return 0

    @pl.when(taker)
    def _():
        squares = jnp.zeros((1, HD), f32)
        for n in range(2):
            send(rs_recv.at[n], rs_recv.at[n], rs_s.at[n], rs_r.at[n], sib).wait_recv()
            total = rs_recv[n, 0].astype(f32)
            for i in range(1, Z * X):
                total += rs_recv[n, i].astype(f32)
            wsum[n] = total
            squares += jnp.sum(total * total, axis=0, keepdims=True)
        cp_w.start()
        sq1[0] = squares
        lax.fori_loop(1, Y * X, send_xy, 0)
        all_xy.wait_recv()
        sq2[z] = jnp.sum(sq1[...], axis=0)
        lax.fori_loop(0, Z * C, send_zc, 0)
        some_zc.wait_recv()

    @pl.when(jnp.logical_not(taker))
    def _():
        cp_w.wait_recv()
        all_zc.wait_recv()

    def sums_left():
        @pl.when(taker)
        def _():
            cp_w.wait_send()
            all_xy.wait_send()
            for part in (pl.ds(0, Z), pl.ds(0, Z - 1)):
                send(sq2.at[part], sq2.at[part], sq_s.at[1], sq_r.at[1], sib).wait_send()

    late.append(sums_left)
    parts = []
    for k in range(C):
        at = pl.ds(k * ROWS, ROWS)
        parts.append(jnp.concatenate([wsum[1, at, :], wsum[0, at, :]], axis=1))
    rows_sum = jnp.where(c == 0, parts[0], parts[1])

    lanes = jnp.sum(sq2[...], axis=0)
    square_total = jnp.sum(lanes, axis=1, keepdims=True)
    limit = math.sqrt(D * 2 * HD)
    clip = jnp.minimum(1.0, limit / (jnp.sqrt(square_total) + 1e-6))
    w_ref[...] = rows_sum * clip

    for copy in [cp_q, cp_do, cp_st, *cp_k, *cp_v, *cp_x, *cp_ret, cp_dq, *cp_g, *cp_ex]:
        copy.wait_send()

    for wait in late:
        wait()


def on_device(queries, keys, values, attention_out, output_grad, log_norm, layer_input, doc_start, visible_blocks):
    hbm = pl.BlockSpec(memory_space=pl.ANY)
    dma = pltpu.SemaphoreType.DMA
    return pl.pallas_call(
        kernel,
        out_shape=(pltpu.VMEM((ROWS, 2 * HD), f32), pltpu.VMEM((T, HQ * HD), bf16)),
        in_specs=[hbm] * 9,
        out_specs=(pl.BlockSpec(memory_space=pltpu.VMEM),) * 2,
        scratch_shapes=[
            pltpu.VMEM((HQ, T), f32),
            pltpu.VMEM((1, T), jnp.int32),
            pltpu.VMEM((1, 5), jnp.int32),
            pltpu.VMEM((C, T, HQ * HD), bf16),
            pltpu.VMEM((C, T, HQ * HD), bf16),
            pltpu.VMEM((T, HQ * HD), bf16),
            pltpu.VMEM((3, T, HD), bf16),
            pltpu.VMEM((3, T, HD), bf16),
            pltpu.VMEM((C, 16, T), f32),
            pltpu.VMEM((3, HQ, T, 2 * T), f32),
            pltpu.VMEM((HQ, 3 * T, 2 * T), bf16),
            pltpu.VMEM((4, T, HD), bf16),
            pltpu.VMEM((4, T, HD), bf16),
            pltpu.VMEM((C, T, HQ * HD), f32),
            pltpu.VMEM((T, HQ * HD), f32),
            pltpu.VMEM((GROUP, T, UNIT), bf16),
            pltpu.VMEM((C, HALF, GROUP * T), bf16),
            pltpu.VMEM((2, T, HD), f32),
            pltpu.VMEM((2, GROUP, T, HD), bf16),
            pltpu.VMEM((HALF, HD), f32),
            pltpu.VMEM((2, HALF, HD), bf16),
            pltpu.VMEM((2, HALF, HD), bf16),
            pltpu.VMEM((2, Z // C * X, MSG, HD), bf16),
            pltpu.VMEM((2, Z * X, MSG, HD), bf16),
            pltpu.VMEM((2, MSG, HD), f32),
            pltpu.VMEM((Y * X, 1, HD), f32),
            pltpu.VMEM((Z, 1, HD), f32),
            dma((9,)),
            dma((3,)),
            dma((3,)),
            dma((4,)),
            dma((4,)),
            dma((4,)),
            dma((4,)),
            dma((3,)),
            dma((3,)),
            dma((2, 3)),
            dma((2, 3)),
            dma((1,)),
            dma((1,)),
            dma((2,)),
            dma((2,)),
            dma((2,)),
            dma((2,)),
            dma((1,)),
            dma((1,)),
            dma((2,)),
            dma((2,)),
        ],
        compiler_params=pltpu.CompilerParams(
            collective_id=0, has_side_effects=True, vmem_limit_bytes=56 * 2**20
        ),
        name="clip_attention_backward",
    )(
        queries,
        keys,
        values,
        attention_out,
        output_grad,
        log_norm,
        layer_input,
        doc_start.reshape(1, T),
        visible_blocks,
    )


def solution(mesh):
    both = ("inner", "outer")
    return jax.shard_map(
        on_device,
        mesh=mesh,
        in_specs=(
            P(both, None),
            P(both, None),
            P(both, None),
            P(both, None),
            P(both, None),
            P(None, both),
            P(both, None),
            P(both),
            P(both, None),
        ),
        out_specs=(P(both, None), P(both, None)),
        check_vma=False,
    )
```

time: 57.7 us -> 54.4 us (0.943)
  Pallas kernels: 55.7 us -> 52.4 us
    pallas_call x1, Pallas kernels: 55.7 us -> 52.4 us  [on_device(): pl.pallas_call(kernel, out_shape=(pltpu.VMEM((ROWS, 2 * HD), f32), pltpu....]
where the time goes in v3:
time: 54.4 us; the launch traced here: 54.3 us
  Pallas kernels  52.4 us (96%)
  local copies, waits for them, and re-layouts  1.28 us (2%)
  between operations  0.64 us (1%)
    pallas_call x1, Pallas kernels, on_device(): pl.pallas_call(kernel, out_shape=(pltpu.VMEM((ROWS, 2 * HD), f32), pltpu....  52.4 us
    unnamed x2, local copies, waits for them, and re-layouts  1.28 us

profile of v3, /device:TPU:1, one launch (start us, length us, event | category | flops | bytes accessed | tf_op | source)
XLA Modules:
  0.0 54.3 jit_solution(3006515416145779404)
XLA Ops:
  0.6 52.4 %clip_attention_backward.1 = (f32[20,256]{1,0:T(8,128)S(1)}, bf16[128,640]{1,0:T(8,128)(2,1)S(1)}) custom-call(bf16[128,640]{1,0:T(8,128)(2,1)} %q_hbm.1, bf16[128,128]{1,0:T(8,128)(2,1)} %k_hbm.1, bf16[128,128]{1,0:T(8,128)(2,1)} %v_hbm.1, bf16[128,640]{1,0:T(8,128)(2,1)} %o_hbm.1, bf16[128,640]{1,0:T(8,128)(2,1)} %do_hbm.1, f32[5,128]{1,0:T(8,128)} %lse_hbm.1, ...), custom_call_target="tpu_custom_call" | custom-call | tf_op jit(solution)/shard_map/clip_attention_backward/pallas_call | solution.py:423
  53.0 0.6 %copy.13 = f32[20,256]{1,0:T(8,128)} copy(f32[20,256]{1,0:T(8,128)S(1)} %get-tuple-element.2) | data formatting | bytes 40960
  53.6 0.7 %copy.14 = bf16[128,640]{1,0:T(8,128)(2,1)} copy(bf16[128,640]{1,0:T(8,128)(2,1)S(1)} %get-tuple-element.3) | data formatting | bytes 327680

commit v4 on v3

--- a/solution.py
+++ b/solution.py
@@ -18,7 +18,6 @@
 HALF = UNIT // C
 ROWS = D // N
 PAIR = C * ROWS
-MSG = 48
 FAR = 1.0e9
 MESH = pl.DeviceIdType.MESH
 f32, bf16 = jnp.float32, jnp.bfloat16
@@ -94,6 +93,7 @@
     w_r,
     sq_s,
     sq_r,
+    wave,
 ):
     y = lax.axis_index("inner")
     outer = lax.axis_index("outer")
@@ -104,7 +104,6 @@
     block = y * (Z * X * C) + outer
     sib = place(y, z, x, other)
     taker = z // (Z // C) == c
-    one = jnp.where(taker, 1, 0)
     ay, az = lax.rem(y, 2), lax.rem(z, 2)
     pair_y = lax.rem(y + jnp.where(ay == c, 1, Y - 1), Y)
     pair_z = lax.rem(z + jnp.where(az == c, 1, Z - 1), Z)
@@ -127,6 +126,27 @@
             src_ref=src, dst_ref=dst, send_sem=ssem, recv_sem=rsem, device_id=device, device_id_type=MESH
         )
         return copy
+
+    barrier = pltpu.get_barrier_semaphore()
+
+    def greet(device):
+        pl.semaphore_signal(barrier, inc=1, device_id=device, device_id_type=MESH)
+
+    z_steps = [[place(y, lax.rem(z + dz, Z), x, c) for dz in dzs] for dzs in ((1, Z - 1), (2, Z - 2))]
+    x_steps = [place(y, z, lax.rem(x + dx, X), c) for dx in range(1, X)]
+    y_steps = [place(lax.rem(y + dy, Y), z, x, c) for dy in (1, Y - 1)]
+    waves = [z_steps[0], z_steps[1], x_steps, y_steps]
+    near = [sib, *[block_at(step) for step in (-4, 4, -2, 2)], *z_steps[0], *x_steps, *y_steps]
+    near.append(place(pair_y, pair_z, x, c))
+    for device in near:
+        greet(device)
+
+    def wave_out(k):
+        for device in waves[k]:
+            pl.semaphore_signal(wave.at[k], inc=1, device_id=device, device_id_type=MESH)
+
+    def wave_in(k):
+        pl.semaphore_wait(wave.at[k], len(waves[k]))
 
     late = []
     loads = [
@@ -142,45 +162,28 @@
     for load in loads:
         load.start()
 
-    barrier = pltpu.get_barrier_semaphore()
-
-    def greet(device):
-        pl.semaphore_signal(barrier, inc=1, device_id=device, device_id_type=MESH)
-
-    def greet_sources(i, _):
-        yy = 1 - ay + 2 * (i // (Z // 2 * X))
-        zz = y // 2 + 2 * lax.rem(i // X, Z // 2)
-        greet(place(yy, zz, lax.rem(i, X), c))
-        return 0
-
-    def greet_xy(i, _):
-        greet(place(lax.rem(y + i // X, Y), z, lax.rem(x + lax.rem(i, X), X), c))
-        return 0
-
-    def greet_z(zz, _):
-        cc = zz // (Z // C)
-
-        @pl.when((zz != z) | (cc != c))
-        def _():
-            greet(place(y, zz, x, cc))
-
-        return 0
-
-    @pl.when(taker)
-    def _():
-        lax.fori_loop(0, Z * X, greet_sources, 0)
-
-    lax.fori_loop(0, Z, greet_z, 0)
-
-    @pl.when(taker)
-    def _():
-        lax.fori_loop(1, Y * X, greet_xy, 0)
-
-    for step in (-4, 4, -2, 2):
-        greet(block_at(step))
-    for yy, zz in peers:
-        greet(place(yy, zz, x, c))
-    greet(sib)
+    pl.semaphore_wait(barrier, len(near))
+
+    cp_q = send(q_hbm, q_all.at[c], qx_s.at[0], qx_r.at[0], sib)
+    cp_do = send(do_hbm, do_all.at[c], qx_s.at[1], qx_r.at[1], sib)
+    cp_st = send(stat.at[c], stat.at[c], qx_s.at[2], qx_r.at[2], sib)
+    cp_k, cp_v = [
+        [send(src, buf.at[j], kv_s.at[2 * n + j - 1], kv_r.at[2 * n + j - 1], block_at(2 * j)) for j in (1, 2)]
+        for n, (src, buf) in enumerate(((k_hbm, kbuf), (v_hbm, vbuf)))
+    ]
+    for copy in [*cp_k, cp_q, cp_do, *cp_v]:
+        copy.start()
+
+    def x_cols(yy, zz):
+        return x_hbm.at[:, pl.ds(pl.multiple_of(unit_owner(yy, zz) * UNIT, HD), UNIT)]
+
+    x_own = pltpu.make_async_copy(x_cols(y, z), x_recv.at[me], load_sem.at[5])
+    x_own.start()
+    cp_x = []
+    for i, (yy, zz) in enumerate(peers):
+        copy = send(x_cols(yy, zz), x_recv.at[me], x_s.at[i], x_r.at[i], place(yy, zz, x, c))
+        copy.start()
+        cp_x.append(copy)
 
     for i in (0, 1, 5, 6, 7):
         loads[i].wait()
@@ -196,30 +199,8 @@
         hit = jnp.max(jnp.where(vis_ref[...] == wanted, 1.0, 0.0), axis=1, keepdims=True)
         stat[c, pl.ds(10 + d, 1), :] = jnp.where(hit > 0.5, first, FAR)
     stat[c, pl.ds(15, 1), :] = jnp.full((1, T), FAR, f32)
-
-    always = 1 + 4 + 3 + Z // C * X
-    pl.semaphore_wait(barrier, always + one * (Y * X - 1 + Z * C - 1))
-
-    cp_q = send(q_hbm, q_all.at[c], qx_s.at[0], qx_r.at[0], sib)
-    cp_do = send(do_hbm, do_all.at[c], qx_s.at[1], qx_r.at[1], sib)
-    cp_st = send(stat.at[c], stat.at[c], qx_s.at[2], qx_r.at[2], sib)
-    cp_k, cp_v = [
-        [send(src, buf.at[j], kv_s.at[2 * n + j - 1], kv_r.at[2 * n + j - 1], block_at(2 * j)) for j in (1, 2)]
-        for n, (src, buf) in enumerate(((k_hbm, kbuf), (v_hbm, vbuf)))
-    ]
-    for copy in [*cp_k, cp_st, cp_q, cp_do, *cp_v]:
-        copy.start()
-
-    def x_cols(yy, zz):
-        return x_hbm.at[:, pl.ds(pl.multiple_of(unit_owner(yy, zz) * UNIT, HD), UNIT)]
-
-    x_own = pltpu.make_async_copy(x_cols(y, z), x_recv.at[me], load_sem.at[5])
-    x_own.start()
-    cp_x = []
-    for i, (yy, zz) in enumerate(peers):
-        copy = send(x_cols(yy, zz), x_recv.at[me], x_s.at[i], x_r.at[i], place(yy, zz, x, c))
-        copy.start()
-        cp_x.append(copy)
+    cp_st.start()
+    wave_out(0)
 
     for load in loads[2:5]:
         load.wait()
@@ -275,6 +256,8 @@
     cp_ret = []
     own[0] = probs(0)
     own[1] = score_grads(0)
+    wave_in(0)
+    wave_out(1)
     for j in (1, 2):
         cp_k[j - 1].wait_recv()
         cp_ret.append(give_back(0, j, probs(j)))
@@ -282,6 +265,8 @@
         cp_v[j - 1].wait_recv()
         cp_ret.append(give_back(1, j, score_grads(j)))
 
+    wave_in(1)
+    wave_out(2)
     key_cat = kbuf[...].reshape(3 * T, HD)
     for h in range(HQ):
         part = dot(ds_buf[h], key_cat, ((0,), (0,)))
@@ -290,6 +275,8 @@
     cp_dq = send(dq_part.at[other], dq_recv, dq_s.at[0], dq_r.at[0], sib)
     cp_dq.start()
 
+    wave_in(2)
+    wave_out(3)
     x_own.wait()
     for copy in cp_x:
         copy.wait_recv()
@@ -311,39 +298,35 @@
     cp_dq.wait_recv()
     dq_ref[...] = (dq_part[c] + dq_recv[...]).astype(bf16)
 
+    for copy in cp_g:
+        copy.wait_recv()
+    grads = jnp.concatenate([g_all[1].reshape(GROUP * T, HD), g_all[0].reshape(GROUP * T, HD)], axis=1)
+    part_rows = PAIR * X
+    cp_ex = []
+    for kz in range(Z // C):
+        ex_send[kz] = dot(xt[other, pl.ds(kz * part_rows, part_rows), :], grads, ((1,), (0,))).astype(bf16)
+        copy = send(ex_send.at[kz], ex_recv.at[kz], ex_s.at[kz], ex_r.at[kz], sib)
+        copy.start()
+        cp_ex.append(copy)
+    for kz in range(Z // C):
+        acc[kz] = dot(xt[c, pl.ds(kz * part_rows, part_rows), :], grads, ((1,), (0,)))
+    wave_in(3)
     slot = (y // 2 * (Z // 2) + z // 2) * X + x
     to_y = unit_owner(y, z)
-    part_rows = PAIR * X
-    cp_ex = []
-    for n in range(2):
-        for copy in cp_g[3 * n : 3 * n + 3]:
-            copy.wait_recv()
-        grads = g_all[n].reshape(GROUP * T, HD)
-        ex_send[n] = dot(xt[other], grads, ((1,), (0,))).astype(bf16)
-        copy = send(ex_send.at[n], ex_recv.at[n], ex_s.at[n], ex_r.at[n], sib)
-        copy.start()
-        cp_ex.append(copy)
-        acc[...] = dot(xt[c], grads, ((1,), (0,)))
-        copy.wait_recv()
-        for kz in range(Z // C):
-            rows = pl.ds(kz * part_rows, part_rows)
-            acc[rows, :] += ex_recv[n, rows, :].astype(f32)
-            for kx in range(X):
-                m = kz * X + kx
-                part = jnp.concatenate([acc[pl.ds(m * PAIR, PAIR), :], jnp.zeros((MSG - PAIR, HD), f32)], axis=0)
-                rs_send[n, m] = part.astype(bf16)
-                send(
-                    rs_send.at[n, m],
-                    rs_recv.at[n, slot],
-                    rs_s.at[n],
-                    rs_r.at[n],
-                    place(to_y, c * (Z // C) + kz, kx, c),
-                ).start()
+    for kz in range(Z // C):
+        cp_ex[kz].wait_recv()
+        acc[kz] += ex_recv[kz].astype(f32)
+        for kx in range(X):
+            at = pl.ds(kx * PAIR, PAIR)
+            part = jnp.concatenate([acc[kz, at, pl.ds(0, HD)], acc[kz, at, pl.ds(HD, HD)]], axis=0)
+            m = kz * X + kx
+            rs_send[m] = part.astype(bf16)
+            to = place(to_y, c * (Z // C) + kz, kx, c)
+            send(rs_send.at[m], rs_recv.at[slot], rs_s.at[0], rs_r.at[0], to).start()
 
     def rs_left():
-        for n in range(2):
-            whole = rs_recv.at[n, pl.ds(0, Z // C * X)]
-            send(rs_send.at[n], whole, rs_s.at[n], rs_r.at[n], sib).wait_send()
+        whole = rs_recv.at[pl.ds(0, Z // C * X)]
+        send(rs_send, whole, rs_s.at[0], rs_r.at[0], sib).wait_send()
 
     late.append(rs_left)
     cp_w = send(wsum, wsum, w_s.at[0], w_r.at[0], sib)
@@ -368,16 +351,13 @@
 
     @pl.when(taker)
     def _():
-        squares = jnp.zeros((1, HD), f32)
-        for n in range(2):
-            send(rs_recv.at[n], rs_recv.at[n], rs_s.at[n], rs_r.at[n], sib).wait_recv()
-            total = rs_recv[n, 0].astype(f32)
-            for i in range(1, Z * X):
-                total += rs_recv[n, i].astype(f32)
-            wsum[n] = total
-            squares += jnp.sum(total * total, axis=0, keepdims=True)
+        send(rs_recv, rs_recv, rs_s.at[0], rs_r.at[0], sib).wait_recv()
+        total = rs_recv[0].astype(f32)
+        for i in range(1, Z * X):
+            total += rs_recv[i].astype(f32)
+        wsum[...] = total
         cp_w.start()
-        sq1[0] = squares
+        sq1[0] = jnp.sum(total * total, axis=0, keepdims=True)
         lax.fori_loop(1, Y * X, send_xy, 0)
         all_xy.wait_recv()
         sq2[z] = jnp.sum(sq1[...], axis=0)
@@ -400,8 +380,8 @@
     late.append(sums_left)
     parts = []
     for k in range(C):
-        at = pl.ds(k * ROWS, ROWS)
-        parts.append(jnp.concatenate([wsum[1, at, :], wsum[0, at, :]], axis=1))
+        at, then = pl.ds(k * ROWS, ROWS), pl.ds(PAIR + k * ROWS, ROWS)
+        parts.append(jnp.concatenate([wsum[at, :], wsum[then, :]], axis=1))
     rows_sum = jnp.where(c == 0, parts[0], parts[1])
 
     lanes = jnp.sum(sq2[...], axis=0)
@@ -445,12 +425,12 @@
             pltpu.VMEM((C, HALF, GROUP * T), bf16),
             pltpu.VMEM((2, T, HD), f32),
             pltpu.VMEM((2, GROUP, T, HD), bf16),
-            pltpu.VMEM((HALF, HD), f32),
-            pltpu.VMEM((2, HALF, HD), bf16),
-            pltpu.VMEM((2, HALF, HD), bf16),
-            pltpu.VMEM((2, Z // C * X, MSG, HD), bf16),
-            pltpu.VMEM((2, Z * X, MSG, HD), bf16),
-            pltpu.VMEM((2, MSG, HD), f32),
+            pltpu.VMEM((Z // C, PAIR * X, 2 * HD), f32),
+            pltpu.VMEM((Z // C, PAIR * X, 2 * HD), bf16),
+            pltpu.VMEM((Z // C, PAIR * X, 2 * HD), bf16),
+            pltpu.VMEM((Z // C * X, 2 * PAIR, HD), bf16),
+            pltpu.VMEM((Z * X, 2 * PAIR, HD), bf16),
+            pltpu.VMEM((2 * PAIR, HD), f32),
             pltpu.VMEM((Y * X, 1, HD), f32),
             pltpu.VMEM((Z, 1, HD), f32),
             dma((9,)),
@@ -466,14 +446,15 @@
             dma((2, 3)),
             dma((1,)),
             dma((1,)),
+            dma((Z // C,)),
+            dma((Z // C,)),
+            dma((1,)),
+            dma((1,)),
+            dma((1,)),
+            dma((1,)),
             dma((2,)),
             dma((2,)),
-            dma((2,)),
-            dma((2,)),
-            dma((1,)),
-            dma((1,)),
-            dma((2,)),
-            dma((2,)),
+            pltpu.SemaphoreType.REGULAR((4,)),
         ],
         compiler_params=pltpu.CompilerParams(
             collective_id=0, has_side_effects=True, vmem_limit_bytes=56 * 2**20

time: 54.4 us -> 52 us (0.956)
  Pallas kernels: 52.4 us -> 50 us
    pallas_call x1, Pallas kernels: 52.4 us -> 50 us  [on_device(): pl.pallas_call(kernel, out_shape=(pltpu.VMEM((ROWS, 2 * HD), f32), pltpu....]
where the time goes in v4:
time: 52 us; the launch traced here: 51.9 us
  Pallas kernels  50 us (96%)
  local copies, waits for them, and re-layouts  1.28 us (2%)
  between operations  0.64 us (1%)
    pallas_call x1, Pallas kernels, on_device(): pl.pallas_call(kernel, out_shape=(pltpu.VMEM((ROWS, 2 * HD), f32), pltpu....  50 us
    unnamed x2, local copies, waits for them, and re-layouts  1.28 us

profile of v4, /device:TPU:1, one launch (start us, length us, event | category | flops | bytes accessed | tf_op | source)
XLA Modules:
  0.0 51.9 jit_solution(1873875150522742600)
XLA Ops:
  0.6 50.0 %clip_attention_backward.1 = (f32[20,256]{1,0:T(8,128)S(1)}, bf16[128,640]{1,0:T(8,128)(2,1)S(1)}) custom-call(bf16[128,640]{1,0:T(8,128)(2,1)} %q_hbm.1, bf16[128,128]{1,0:T(8,128)(2,1)} %k_hbm.1, bf16[128,128]{1,0:T(8,128)(2,1)} %v_hbm.1, bf16[128,640]{1,0:T(8,128)(2,1)} %o_hbm.1, bf16[128,640]{1,0:T(8,128)(2,1)} %do_hbm.1, f32[5,128]{1,0:T(8,128)} %lse_hbm.1, ...), custom_call_target="tpu_custom_call" | custom-call | tf_op jit(solution)/shard_map/clip_attention_backward/pallas_call | solution.py:403
  50.7 0.6 %copy.13 = f32[20,256]{1,0:T(8,128)} copy(f32[20,256]{1,0:T(8,128)S(1)} %get-tuple-element.2) | data formatting | bytes 40960
  51.3 0.7 %copy.14 = bf16[128,640]{1,0:T(8,128)(2,1)} copy(bf16[128,640]{1,0:T(8,128)(2,1)S(1)} %get-tuple-element.3) | data formatting | bytes 327680

commit v5 on v4

--- a/solution.py
+++ b/solution.py
@@ -18,6 +18,7 @@
 HALF = UNIT // C
 ROWS = D // N
 PAIR = C * ROWS
+EARLY = 32
 FAR = 1.0e9
 MESH = pl.DeviceIdType.MESH
 f32, bf16 = jnp.float32, jnp.bfloat16
@@ -55,6 +56,7 @@
     vbuf,
     stat,
     p_buf,
+    p_half,
     ds_buf,
     ret_send,
     ret_recv,
@@ -104,18 +106,11 @@
     block = y * (Z * X * C) + outer
     sib = place(y, z, x, other)
     taker = z // (Z // C) == c
-    ay, az = lax.rem(y, 2), lax.rem(z, 2)
-    pair_y = lax.rem(y + jnp.where(ay == c, 1, Y - 1), Y)
-    pair_z = lax.rem(z + jnp.where(az == c, 1, Z - 1), Z)
-    peers = [(pair_y, z), (y, pair_z), (pair_y, pair_z)]
-
-    def member(yy, zz):
-        return 2 * lax.rem(yy, 2) + lax.rem(zz, 2)
+    dz = jnp.where(c == 0, 1, Z - 1)
+    peers = [(lax.rem(y + 1, Y), z), (lax.rem(y + Y - 1, Y), z), (y, lax.rem(z + dz, Z))]
 
     def unit_owner(yy, zz):
-        return 1 - lax.rem(yy, 2) + 2 * lax.rem(zz, 2)
-
-    me = member(y, z)
+        return lax.rem(yy + 2 * zz + 1, Y)
 
     def block_at(step):
         b = lax.rem(block + (step + N), N)
@@ -137,7 +132,6 @@
     y_steps = [place(lax.rem(y + dy, Y), z, x, c) for dy in (1, Y - 1)]
     waves = [z_steps[0], z_steps[1], x_steps, y_steps]
     near = [sib, *[block_at(step) for step in (-4, 4, -2, 2)], *z_steps[0], *x_steps, *y_steps]
-    near.append(place(pair_y, pair_z, x, c))
     for device in near:
         greet(device)
 
@@ -177,11 +171,11 @@
     def x_cols(yy, zz):
         return x_hbm.at[:, pl.ds(pl.multiple_of(unit_owner(yy, zz) * UNIT, HD), UNIT)]
 
-    x_own = pltpu.make_async_copy(x_cols(y, z), x_recv.at[me], load_sem.at[5])
+    x_own = pltpu.make_async_copy(x_cols(y, z), x_recv.at[0], load_sem.at[5])
     x_own.start()
     cp_x = []
     for i, (yy, zz) in enumerate(peers):
-        copy = send(x_cols(yy, zz), x_recv.at[me], x_s.at[i], x_r.at[i], place(yy, zz, x, c))
+        copy = send(x_cols(yy, zz), x_recv.at[1 + i], x_s.at[i], x_r.at[i], place(yy, zz, x, c))
         copy.start()
         cp_x.append(copy)
 
@@ -211,59 +205,69 @@
     def row(r):
         return jnp.concatenate([stat[0, pl.ds(r, 1), :], stat[1, pl.ds(r, 1), :]], axis=1)
 
-    iota_u = lax.broadcasted_iota(jnp.int32, (T, 2 * T), 0)
-    iota_t = lax.broadcasted_iota(jnp.int32, (T, 2 * T), 1)
-    pair_first = (block - c) * T
-    query_pos = pair_first + iota_t
-
-    def probs(j):
-        key_pos = (block - 2 * j) * T + iota_u
+
+    def lowest(j):
         lows = []
         for i in range(C):
             d0, d1 = i + 2 * j, i - 1 + 2 * j
             at0, at1 = 10 + min(d0, 5), 10 + (d1 if d1 >= 0 else 5)
             lows.append(jnp.where(c == 0, stat[i, pl.ds(at0, 1), :], stat[i, pl.ds(at1, 1), :]))
-        low = jnp.concatenate(lows, axis=1)
-        allowed = (key_pos.astype(f32) >= low) & (key_pos <= query_pos)
-        key_rows = kbuf[j]
-        part = jnp.zeros((T, HD), f32)
+        return jnp.concatenate(lows, axis=1)
+
+    def heads(ref, h):
+        return ref[:, :, pl.ds(h * HD, HD)].reshape(2 * T, HD)
+
+    def probs(first, count):
+        rows = pl.ds(first * T, count * T)
+        iota_u = lax.broadcasted_iota(jnp.int32, (count * T, 2 * T), 0)
+        iota_t = lax.broadcasted_iota(jnp.int32, (count * T, 2 * T), 1)
+        key_pos = (block - 2 * first) * T + iota_u
+        low = lowest(first)
+        if count == 2:
+            key_pos = jnp.where(iota_u < T, key_pos, key_pos - 3 * T)
+            low = jnp.where(iota_u < T, low, lowest(first + 1))
+        allowed = (key_pos.astype(f32) >= low) & (key_pos <= (block - c) * T + iota_t)
+        key_rows = kbuf[first : first + count].reshape(count * T, HD)
         for h in range(HQ):
-            cols = pl.ds(h * HD, HD)
-            s = dot(key_rows, q_all[:, :, cols].reshape(2 * T, HD), ((1,), (1,)))
+            s = dot(key_rows, heads(q_all, h), ((1,), (1,)))
             prob = jnp.where(allowed, jnp.exp2(s * (SCALE * LOG2E) - row(HQ + h)), 0.0)
-            p_buf[j, h] = prob
-            part += dot(prob.astype(bf16), do_all[:, :, cols].reshape(2 * T, HD), ((1,), (0,)))
+            p_buf[h, rows, :] = prob
+            p_half[h, rows, :] = prob.astype(bf16)
+        part = jnp.zeros((count * T, HD), f32)
+        for h in range(HQ):
+            part += dot(p_half[h, rows, :], heads(do_all, h), ((1,), (0,)))
         return part
 
-    def score_grads(j):
-        value_rows = vbuf[j]
-        part = jnp.zeros((T, HD), f32)
+    def score_grads(first, count):
+        rows = pl.ds(first * T, count * T)
+        value_rows = vbuf[first : first + count].reshape(count * T, HD)
         for h in range(HQ):
-            cols = pl.ds(h * HD, HD)
-            dp = dot(value_rows, do_all[:, :, cols].reshape(2 * T, HD), ((1,), (1,)))
-            ds = (p_buf[j, h] * (dp - row(h)) * SCALE).astype(bf16)
-            ds_buf[h, pl.ds(j * T, T), :] = ds
-            part += dot(ds, q_all[:, :, cols].reshape(2 * T, HD), ((1,), (0,)))
+            dp = dot(value_rows, heads(do_all, h), ((1,), (1,)))
+            ds_buf[h, rows, :] = (p_buf[h, rows, :] * (dp - row(h)) * SCALE).astype(bf16)
+        part = jnp.zeros((count * T, HD), f32)
+        for h in range(HQ):
+            part += dot(ds_buf[h, rows, :], heads(q_all, h), ((1,), (0,)))
         return part
 
-    def give_back(n, j, part):
-        k = 2 * n + j - 1
-        ret_send[k] = part.astype(bf16)
-        copy = send(ret_send.at[k], ret_recv.at[k], ret_s.at[k], ret_r.at[k], block_at(-2 * j))
-        copy.start()
-        return copy
+    def give_back(n, part):
+        for j in (2, 1):
+            k = 2 * n + j - 1
+            ret_send[k] = part[(j - 1) * T : j * T].astype(bf16)
+            copy = send(ret_send.at[k], ret_recv.at[k], ret_s.at[k], ret_r.at[k], block_at(-2 * j))
+            copy.start()
+            cp_ret.append(copy)
 
     cp_ret = []
-    own[0] = probs(0)
-    own[1] = score_grads(0)
+    own[0] = probs(0, 1)
+    own[1] = score_grads(0, 1)
     wave_in(0)
     wave_out(1)
-    for j in (1, 2):
-        cp_k[j - 1].wait_recv()
-        cp_ret.append(give_back(0, j, probs(j)))
-    for j in (1, 2):
-        cp_v[j - 1].wait_recv()
-        cp_ret.append(give_back(1, j, score_grads(j)))
+    for copy in cp_k:
+        copy.wait_recv()
+    give_back(0, probs(1, 2))
+    for copy in cp_v:
+        copy.wait_recv()
+    give_back(1, score_grads(1, 2))
 
     wave_in(1)
     wave_out(2)
@@ -275,58 +279,78 @@
     cp_dq = send(dq_part.at[other], dq_recv, dq_s.at[0], dq_r.at[0], sib)
     cp_dq.start()
 
-    wave_in(2)
-    wave_out(3)
+    def transpose(m):
+        for hc in range(C):
+            xt[hc, m] = x_recv[m, :, pl.ds(hc * HALF, HALF)].T
+
     x_own.wait()
-    for copy in cp_x:
-        copy.wait_recv()
-    for m in range(GROUP):
-        for hc in range(C):
-            xt[hc, :, pl.ds(m * T, T)] = x_recv[m, :, pl.ds(hc * HALF, HALF)].T
+    transpose(0)
 
     cp_g = []
     for n in range(2):
         cp_ret[2 * n].wait_recv()
         cp_ret[2 * n + 1].wait_recv()
-        g_all[n, me] = (own[n] + ret_recv[2 * n].astype(f32) + ret_recv[2 * n + 1].astype(f32)).astype(bf16)
-        mine = g_all.at[n, me]
-        for i, (yy, zz) in reversed(list(enumerate(peers))):
-            copy = send(mine, mine, g_s.at[n, i], g_r.at[n, i], place(yy, zz, x, c))
+        g_all[n, 0] = (own[n] + ret_recv[2 * n].astype(f32) + ret_recv[2 * n + 1].astype(f32)).astype(bf16)
+        for i, (yy, zz) in enumerate(peers):
+            copy = send(g_all.at[n, 0], g_all.at[n, 1 + i], g_s.at[n, i], g_r.at[n, i], place(yy, zz, x, c))
             copy.start()
             cp_g.append(copy)
-
-    cp_dq.wait_recv()
-    dq_ref[...] = (dq_part[c] + dq_recv[...]).astype(bf16)
-
-    for copy in cp_g:
-        copy.wait_recv()
-    grads = jnp.concatenate([g_all[1].reshape(GROUP * T, HD), g_all[0].reshape(GROUP * T, HD)], axis=1)
-    part_rows = PAIR * X
+        if n == 0:
+            wave_in(2)
+            wave_out(3)
+            cp_dq.wait_recv()
+            dq_ref[...] = (dq_part[c] + dq_recv[...]).astype(bf16)
+
+    for i in range(GROUP - 1):
+        cp_x[i].wait_recv()
+        transpose(1 + i)
+
+    slot = z * X + x
+    to_y = unit_owner(y, z)
+    parts = 2
+    step = HALF // parts
     cp_ex = []
-    for kz in range(Z // C):
-        ex_send[kz] = dot(xt[other, pl.ds(kz * part_rows, part_rows), :], grads, ((1,), (0,))).astype(bf16)
-        copy = send(ex_send.at[kz], ex_recv.at[kz], ex_s.at[kz], ex_r.at[kz], sib)
-        copy.start()
-        cp_ex.append(copy)
-    for kz in range(Z // C):
-        acc[kz] = dot(xt[c, pl.ds(kz * part_rows, part_rows), :], grads, ((1,), (0,)))
-    wave_in(3)
-    slot = (y // 2 * (Z // 2) + z // 2) * X + x
-    to_y = unit_owner(y, z)
-    for kz in range(Z // C):
-        cp_ex[kz].wait_recv()
-        acc[kz] += ex_recv[kz].astype(f32)
-        for kx in range(X):
-            at = pl.ds(kx * PAIR, PAIR)
-            part = jnp.concatenate([acc[kz, at, pl.ds(0, HD)], acc[kz, at, pl.ds(HD, HD)]], axis=0)
-            m = kz * X + kx
-            rs_send[m] = part.astype(bf16)
-            to = place(to_y, c * (Z // C) + kz, kx, c)
-            send(rs_send.at[m], rs_recv.at[slot], rs_s.at[0], rs_r.at[0], to).start()
+
+    def product(hc, n, rows):
+        total = dot(xt[hc, 0, rows, :], g_all[n, 0], ((1,), (0,)))
+        for m in range(1, GROUP):
+            total += dot(xt[hc, m, rows, :], g_all[n, m], ((1,), (0,)))
+        return total
+
+    for n in range(2):
+        for copy in cp_g[3 * n : 3 * n + 3]:
+            copy.wait_recv()
+        for p in range(parts):
+            ex_send[n, p] = product(other, n, pl.ds(p * step, step)).astype(bf16)
+            copy = send(ex_send.at[n, p], ex_recv.at[n, p], ex_s.at[n, p], ex_r.at[n, p], sib)
+            copy.start()
+            cp_ex.append(copy)
+        for p in range(parts):
+            acc[n, pl.ds(p * step, step), :] = product(c, n, pl.ds(p * step, step))
+        if n == 0:
+            wave_in(3)
+        for p in range(parts):
+            cp_ex[parts * n + p].wait_recv()
+            acc[n, pl.ds(p * step, step), :] += ex_recv[n, p].astype(f32)
+            for i in range(step // PAIR):
+                m = p * (step // PAIR) + i
+                if n == 0:
+                    rows = pl.ds(0, EARLY)
+                    rs_send[m, rows, :] = acc[0, pl.ds(m * PAIR, EARLY), :].astype(bf16)
+                else:
+                    rows = pl.ds(EARLY, 2 * PAIR - EARLY)
+                    left = acc[0, pl.ds(m * PAIR + EARLY, PAIR - EARLY), :]
+                    both = jnp.concatenate([left, acc[1, pl.ds(m * PAIR, PAIR), :]], axis=0)
+                    rs_send[m, rows, :] = both.astype(bf16)
+                to = place(to_y, c * (Z // C) + m // X, m % X, c)
+                send(rs_send.at[m, rows], rs_recv.at[slot, rows], rs_s.at[n], rs_r.at[n], to).start()
+
+    shares = (pl.ds(0, EARLY), pl.ds(EARLY, 2 * PAIR - EARLY))
 
     def rs_left():
-        whole = rs_recv.at[pl.ds(0, Z // C * X)]
-        send(rs_send, whole, rs_s.at[0], rs_r.at[0], sib).wait_send()
+        for n, rows in enumerate(shares):
+            some = rs_recv.at[pl.ds(0, Z // C * X), rows]
+            send(rs_send.at[:, rows], some, rs_s.at[n], rs_r.at[n], sib).wait_send()
 
     late.append(rs_left)
     cp_w = send(wsum, wsum, w_s.at[0], w_r.at[0], sib)
@@ -351,13 +375,17 @@
 
     @pl.when(taker)
     def _():
-        send(rs_recv, rs_recv, rs_s.at[0], rs_r.at[0], sib).wait_recv()
-        total = rs_recv[0].astype(f32)
-        for i in range(1, Z * X):
-            total += rs_recv[i].astype(f32)
-        wsum[...] = total
+        squares = jnp.zeros((1, HD), f32)
+        for n, rows in enumerate(shares):
+            here = rs_recv.at[:, rows]
+            send(here, here, rs_s.at[n], rs_r.at[n], sib).wait_recv()
+            total = rs_recv[0, rows, :].astype(f32)
+            for i in range(1, Z * X):
+                total += rs_recv[i, rows, :].astype(f32)
+            wsum[rows, :] = total
+            squares += jnp.sum(total * total, axis=0, keepdims=True)
         cp_w.start()
-        sq1[0] = jnp.sum(total * total, axis=0, keepdims=True)
+        sq1[0] = squares
         lax.fori_loop(1, Y * X, send_xy, 0)
         all_xy.wait_recv()
         sq2[z] = jnp.sum(sq1[...], axis=0)
@@ -378,11 +406,11 @@
                 send(sq2.at[part], sq2.at[part], sq_s.at[1], sq_r.at[1], sib).wait_send()
 
     late.append(sums_left)
-    parts = []
+    halves = []
     for k in range(C):
         at, then = pl.ds(k * ROWS, ROWS), pl.ds(PAIR + k * ROWS, ROWS)
-        parts.append(jnp.concatenate([wsum[at, :], wsum[then, :]], axis=1))
-    rows_sum = jnp.where(c == 0, parts[0], parts[1])
+        halves.append(jnp.concatenate([wsum[then, :], wsum[at, :]], axis=1))
+    rows_sum = jnp.where(c == 0, halves[0], halves[1])
 
     lanes = jnp.sum(sq2[...], axis=0)
     square_total = jnp.sum(lanes, axis=1, keepdims=True)
@@ -415,19 +443,20 @@
             pltpu.VMEM((3, T, HD), bf16),
             pltpu.VMEM((3, T, HD), bf16),
             pltpu.VMEM((C, 16, T), f32),
-            pltpu.VMEM((3, HQ, T, 2 * T), f32),
+            pltpu.VMEM((HQ, 3 * T, 2 * T), f32),
+            pltpu.VMEM((HQ, 3 * T, 2 * T), bf16),
             pltpu.VMEM((HQ, 3 * T, 2 * T), bf16),
             pltpu.VMEM((4, T, HD), bf16),
             pltpu.VMEM((4, T, HD), bf16),
             pltpu.VMEM((C, T, HQ * HD), f32),
             pltpu.VMEM((T, HQ * HD), f32),
             pltpu.VMEM((GROUP, T, UNIT), bf16),
-            pltpu.VMEM((C, HALF, GROUP * T), bf16),
+            pltpu.VMEM((C, GROUP, HALF, T), bf16),
             pltpu.VMEM((2, T, HD), f32),
             pltpu.VMEM((2, GROUP, T, HD), bf16),
-            pltpu.VMEM((Z // C, PAIR * X, 2 * HD), f32),
-            pltpu.VMEM((Z // C, PAIR * X, 2 * HD), bf16),
-            pltpu.VMEM((Z // C, PAIR * X, 2 * HD), bf16),
+            pltpu.VMEM((2, HALF, HD), f32),
+            pltpu.VMEM((2, 2, HALF // 2, HD), bf16),
+            pltpu.VMEM((2, 2, HALF // 2, HD), bf16),
             pltpu.VMEM((Z // C * X, 2 * PAIR, HD), bf16),
             pltpu.VMEM((Z * X, 2 * PAIR, HD), bf16),
             pltpu.VMEM((2 * PAIR, HD), f32),
@@ -446,10 +475,10 @@
             dma((2, 3)),
             dma((1,)),
             dma((1,)),
-            dma((Z // C,)),
-            dma((Z // C,)),
-            dma((1,)),
-            dma((1,)),
+            dma((2, 2)),
+            dma((2, 2)),
+            dma((2,)),
+            dma((2,)),
             dma((1,)),
             dma((1,)),
             dma((2,)),

time: 52 us -> 48.7 us (0.937)
  Pallas kernels: 50 us -> 46.7 us
    pallas_call x1, Pallas kernels: 50 us -> 46.7 us  [on_device(): pl.pallas_call(kernel, out_shape=(pltpu.VMEM((ROWS, 2 * HD), f32), pltpu....]
where the time goes in v5:
time: 48.7 us
  Pallas kernels  46.7 us (96%)
  local copies, waits for them, and re-layouts  1.28 us (3%)
  between operations  0.64 us (1%)
    pallas_call x1, Pallas kernels, on_device(): pl.pallas_call(kernel, out_shape=(pltpu.VMEM((ROWS, 2 * HD), f32), pltpu....  46.7 us
    unnamed x2, local copies, waits for them, and re-layouts  1.28 us

profile of v5, /device:TPU:1, one launch (start us, length us, event | category | flops | bytes accessed | tf_op | source)
XLA Modules:
  0.0 48.7 jit_solution(13012892402988555483)
XLA Ops:
  0.6 46.7 %clip_attention_backward.1 = (f32[20,256]{1,0:T(8,128)S(1)}, bf16[128,640]{1,0:T(8,128)(2,1)S(1)}) custom-call(bf16[128,640]{1,0:T(8,128)(2,1)} %q_hbm.1, bf16[128,128]{1,0:T(8,128)(2,1)} %k_hbm.1, bf16[128,128]{1,0:T(8,128)(2,1)} %v_hbm.1, bf16[128,640]{1,0:T(8,128)(2,1)} %o_hbm.1, bf16[128,640]{1,0:T(8,128)(2,1)} %do_hbm.1, f32[5,128]{1,0:T(8,128)} %lse_hbm.1, ...), custom_call_target="tpu_custom_call" | custom-call | tf_op jit(solution)/shard_map/clip_attention_backward/pallas_call | solution.py:431
  47.4 0.6 %copy.13 = f32[20,256]{1,0:T(8,128)} copy(f32[20,256]{1,0:T(8,128)S(1)} %get-tuple-element.2) | data formatting | bytes 40960
  48.0 0.7 %copy.14 = bf16[128,640]{1,0:T(8,128)(2,1)} copy(bf16[128,640]{1,0:T(8,128)(2,1)S(1)} %get-tuple-element.3) | data formatting | bytes 327680

commit v6 on v5

--- a/solution.py
+++ b/solution.py
@@ -67,8 +67,6 @@
     own,
     g_all,
     acc,
-    ex_send,
-    ex_recv,
     rs_send,
     rs_recv,
     wsum,
@@ -87,8 +85,6 @@
     g_r,
     dq_s,
     dq_r,
-    ex_s,
-    ex_r,
     rs_s,
     rs_r,
     w_s,
@@ -107,7 +103,11 @@
     sib = place(y, z, x, other)
     taker = z // (Z // C) == c
     dz = jnp.where(c == 0, 1, Z - 1)
-    peers = [(lax.rem(y + 1, Y), z), (lax.rem(y + Y - 1, Y), z), (y, lax.rem(z + dz, Z))]
+    chips = [(y, z), (lax.rem(y + 1, Y), z), (lax.rem(y + Y - 1, Y), z), (y, lax.rem(z + dz, Z))]
+    peers = [(i, *chips[i], cc) for i in (1, 2, 3) for cc in range(C)]
+    peers.append((0, y, z, other))
+    named = [c * GROUP + i for i in range(GROUP)]
+    arrivals = [other * GROUP, *[cs * GROUP + i for i in (1, 2, 3) for cs in range(C)]]
 
     def unit_owner(yy, zz):
         return lax.rem(yy + 2 * zz + 1, Y)
@@ -131,7 +131,10 @@
     x_steps = [place(y, z, lax.rem(x + dx, X), c) for dx in range(1, X)]
     y_steps = [place(lax.rem(y + dy, Y), z, x, c) for dy in (1, Y - 1)]
     waves = [z_steps[0], z_steps[1], x_steps, y_steps]
-    near = [sib, *[block_at(step) for step in (-4, 4, -2, 2)], *z_steps[0], *x_steps, *y_steps]
+    near = [*[block_at(step) for step in (-4, 4, -2, 2)], *x_steps, *y_steps, *z_steps[0]]
+    near += [place(yy, z, x, other) for yy in (lax.rem(y + 1, Y), lax.rem(y + Y - 1, Y))]
+    near += [place(y, zz, x, other) for zz in (lax.rem(z + 1, Z), lax.rem(z + Z - 1, Z))]
+    near.append(sib)
     for device in near:
         greet(device)
 
@@ -168,14 +171,15 @@
     for copy in [*cp_k, cp_q, cp_do, *cp_v]:
         copy.start()
 
-    def x_cols(yy, zz):
-        return x_hbm.at[:, pl.ds(pl.multiple_of(unit_owner(yy, zz) * UNIT, HD), UNIT)]
-
-    x_own = pltpu.make_async_copy(x_cols(y, z), x_recv.at[0], load_sem.at[5])
+    def x_cols(yy, zz, cc):
+        return x_hbm.at[:, pl.ds(pl.multiple_of(unit_owner(yy, zz) * UNIT + cc * HALF, HD), HALF)]
+
+    x_own = pltpu.make_async_copy(x_cols(y, z, c), x_recv.at[named[0]], load_sem.at[5])
     x_own.start()
     cp_x = []
-    for i, (yy, zz) in enumerate(peers):
-        copy = send(x_cols(yy, zz), x_recv.at[1 + i], x_s.at[i], x_r.at[i], place(yy, zz, x, c))
+    for i, yy, zz, cc in peers:
+        at = named[i]
+        copy = send(x_cols(yy, zz, cc), x_recv.at[at], x_s.at[i * C + cc], x_r.at[at], place(yy, zz, x, cc))
         copy.start()
         cp_x.append(copy)
 
@@ -279,20 +283,15 @@
     cp_dq = send(dq_part.at[other], dq_recv, dq_s.at[0], dq_r.at[0], sib)
     cp_dq.start()
 
-    def transpose(m):
-        for hc in range(C):
-            xt[hc, m] = x_recv[m, :, pl.ds(hc * HALF, HALF)].T
-
-    x_own.wait()
-    transpose(0)
-
     cp_g = []
     for n in range(2):
         cp_ret[2 * n].wait_recv()
         cp_ret[2 * n + 1].wait_recv()
-        g_all[n, 0] = (own[n] + ret_recv[2 * n].astype(f32) + ret_recv[2 * n + 1].astype(f32)).astype(bf16)
-        for i, (yy, zz) in enumerate(peers):
-            copy = send(g_all.at[n, 0], g_all.at[n, 1 + i], g_s.at[n, i], g_r.at[n, i], place(yy, zz, x, c))
+        mine = g_all.at[n, named[0]]
+        g_all[n, named[0]] = (own[n] + ret_recv[2 * n].astype(f32) + ret_recv[2 * n + 1].astype(f32)).astype(bf16)
+        for i, yy, zz, cc in peers:
+            at = named[i]
+            copy = send(mine, g_all.at[n, at], g_s.at[n, i * C + cc], g_r.at[n, at], place(yy, zz, x, cc))
             copy.start()
             cp_g.append(copy)
         if n == 0:
@@ -301,51 +300,40 @@
             cp_dq.wait_recv()
             dq_ref[...] = (dq_part[c] + dq_recv[...]).astype(bf16)
 
-    for i in range(GROUP - 1):
-        cp_x[i].wait_recv()
-        transpose(1 + i)
+    x_own.wait()
+    for at in arrivals:
+        send(x_recv.at[at], x_recv.at[at], x_s.at[0], x_r.at[at], sib).wait_recv()
+    for m in range(C * GROUP):
+        xt[m // 2, :, pl.ds(m % 2 * T, T)] = x_recv[m].T
 
     slot = z * X + x
     to_y = unit_owner(y, z)
-    parts = 2
-    step = HALF // parts
-    cp_ex = []
-
-    def product(hc, n, rows):
-        total = dot(xt[hc, 0, rows, :], g_all[n, 0], ((1,), (0,)))
-        for m in range(1, GROUP):
-            total += dot(xt[hc, m, rows, :], g_all[n, m], ((1,), (0,)))
-        return total
-
+    shares = (pl.ds(0, EARLY), pl.ds(EARLY, 2 * PAIR - EARLY))
+    step = PAIR * X
     for n in range(2):
-        for copy in cp_g[3 * n : 3 * n + 3]:
-            copy.wait_recv()
-        for p in range(parts):
-            ex_send[n, p] = product(other, n, pl.ds(p * step, step)).astype(bf16)
-            copy = send(ex_send.at[n, p], ex_recv.at[n, p], ex_s.at[n, p], ex_r.at[n, p], sib)
-            copy.start()
-            cp_ex.append(copy)
-        for p in range(parts):
-            acc[n, pl.ds(p * step, step), :] = product(c, n, pl.ds(p * step, step))
+        for at in arrivals:
+            send(g_all.at[n, at], g_all.at[n, at], g_s.at[n, 0], g_r.at[n, at], sib).wait_recv()
         if n == 0:
             wave_in(3)
-        for p in range(parts):
-            cp_ex[parts * n + p].wait_recv()
-            acc[n, pl.ds(p * step, step), :] += ex_recv[n, p].astype(f32)
-            for i in range(step // PAIR):
-                m = p * (step // PAIR) + i
+        for i in range(Z // C):
+            kz = lax.rem(z + 2 + i, Z // C)
+            rows = pl.ds(pl.multiple_of(kz * step, step), step)
+            total = dot(xt[0, rows, :], g_all[n, 0:2].reshape(2 * T, HD), ((1,), (0,)))
+            for m in range(2, C * GROUP, 2):
+                total += dot(xt[m // 2, rows, :], g_all[n, m : m + 2].reshape(2 * T, HD), ((1,), (0,)))
+            acc[n, rows, :] = total
+            for k in range(X):
+                kx = lax.rem(x + 2 + k, X)
+                m = kz * X + kx
+                at = pl.multiple_of(m * PAIR, PAIR)
                 if n == 0:
-                    rows = pl.ds(0, EARLY)
-                    rs_send[m, rows, :] = acc[0, pl.ds(m * PAIR, EARLY), :].astype(bf16)
+                    part = acc[0, pl.ds(at, EARLY), :]
                 else:
-                    rows = pl.ds(EARLY, 2 * PAIR - EARLY)
-                    left = acc[0, pl.ds(m * PAIR + EARLY, PAIR - EARLY), :]
-                    both = jnp.concatenate([left, acc[1, pl.ds(m * PAIR, PAIR), :]], axis=0)
-                    rs_send[m, rows, :] = both.astype(bf16)
-                to = place(to_y, c * (Z // C) + m // X, m % X, c)
-                send(rs_send.at[m, rows], rs_recv.at[slot, rows], rs_s.at[n], rs_r.at[n], to).start()
-
-    shares = (pl.ds(0, EARLY), pl.ds(EARLY, 2 * PAIR - EARLY))
+                    left = acc[0, pl.ds(pl.multiple_of(at + EARLY, 8), PAIR - EARLY), :]
+                    part = jnp.concatenate([left, acc[1, pl.ds(at, PAIR), :]], axis=0)
+                rs_send[m, shares[n], :] = part.astype(bf16)
+                to = place(to_y, c * (Z // C) + kz, kx, c)
+                send(rs_send.at[m, shares[n]], rs_recv.at[slot, shares[n]], rs_s.at[n], rs_r.at[n], to).start()
 
     def rs_left():
         for n, rows in enumerate(shares):
@@ -418,7 +406,7 @@
     clip = jnp.minimum(1.0, limit / (jnp.sqrt(square_total) + 1e-6))
     w_ref[...] = rows_sum * clip
 
-    for copy in [cp_q, cp_do, cp_st, *cp_k, *cp_v, *cp_x, *cp_ret, cp_dq, *cp_g, *cp_ex]:
+    for copy in [cp_q, cp_do, cp_st, *cp_k, *cp_v, *cp_x, *cp_ret, cp_dq, *cp_g]:
         copy.wait_send()
 
     for wait in late:
@@ -450,13 +438,11 @@
             pltpu.VMEM((4, T, HD), bf16),
             pltpu.VMEM((C, T, HQ * HD), f32),
             pltpu.VMEM((T, HQ * HD), f32),
-            pltpu.VMEM((GROUP, T, UNIT), bf16),
-            pltpu.VMEM((C, GROUP, HALF, T), bf16),
+            pltpu.VMEM((C * GROUP, T, HALF), bf16),
+            pltpu.VMEM((GROUP, HALF, C * T), bf16),
             pltpu.VMEM((2, T, HD), f32),
-            pltpu.VMEM((2, GROUP, T, HD), bf16),
+            pltpu.VMEM((2, C * GROUP, T, HD), bf16),
             pltpu.VMEM((2, HALF, HD), f32),
-            pltpu.VMEM((2, 2, HALF // 2, HD), bf16),
-            pltpu.VMEM((2, 2, HALF // 2, HD), bf16),
             pltpu.VMEM((Z // C * X, 2 * PAIR, HD), bf16),
             pltpu.VMEM((Z * X, 2 * PAIR, HD), bf16),
             pltpu.VMEM((2 * PAIR, HD), f32),
@@ -469,14 +455,12 @@
             dma((4,)),
             dma((4,)),
             dma((4,)),
-            dma((3,)),
-            dma((3,)),
-            dma((2, 3)),
-            dma((2, 3)),
+            dma((C * GROUP,)),
+            dma((C * GROUP,)),
+            dma((2, C * GROUP)),
+            dma((2, C * GROUP)),
             dma((1,)),
             dma((1,)),
-            dma((2, 2)),
-            dma((2, 2)),
             dma((2,)),
             dma((2,)),
             dma((1,)),

time: 48.7 us -> 48 us (0.986)
  Pallas kernels: 46.7 us -> 46 us
    pallas_call x1, Pallas kernels: 46.7 us -> 46 us  [on_device(): pl.pallas_call(kernel, out_shape=(pltpu.VMEM((ROWS, 2 * HD), f32), pltpu....]
where the time goes in v6:
time: 48 us
  Pallas kernels  46 us (96%)
  local copies, waits for them, and re-layouts  1.28 us (3%)
  between operations  0.64 us (1%)
    pallas_call x1, Pallas kernels, on_device(): pl.pallas_call(kernel, out_shape=(pltpu.VMEM((ROWS, 2 * HD), f32), pltpu....  46 us
    unnamed x2, local copies, waits for them, and re-layouts  1.28 us

profile of v6, /device:TPU:1, one launch (start us, length us, event | category | flops | bytes accessed | tf_op | source)
XLA Modules:
  0.0 48.0 jit_solution(8162884502277480613)
XLA Ops:
  0.6 46.0 %clip_attention_backward.1 = (f32[20,256]{1,0:T(8,128)S(1)}, bf16[128,640]{1,0:T(8,128)(2,1)S(1)}) custom-call(bf16[128,640]{1,0:T(8,128)(2,1)} %q_hbm.1, bf16[128,128]{1,0:T(8,128)(2,1)} %k_hbm.1, bf16[128,128]{1,0:T(8,128)(2,1)} %v_hbm.1, bf16[128,640]{1,0:T(8,128)(2,1)} %o_hbm.1, bf16[128,640]{1,0:T(8,128)(2,1)} %do_hbm.1, f32[5,128]{1,0:T(8,128)} %lse_hbm.1, ...), custom_call_target="tpu_custom_call" | custom-call | tf_op jit(solution)/shard_map/clip_attention_backward/pallas_call | solution.py:419
  46.7 0.6 %copy.13 = f32[20,256]{1,0:T(8,128)} copy(f32[20,256]{1,0:T(8,128)S(1)} %get-tuple-element.2) | data formatting | bytes 40960
  47.3 0.7 %copy.14 = bf16[128,640]{1,0:T(8,128)(2,1)} copy(bf16[128,640]{1,0:T(8,128)(2,1)S(1)} %get-tuple-element.3) | data formatting | bytes 327680

commit v7 on v6

--- a/solution.py
+++ b/solution.py
@@ -347,19 +347,18 @@
     some_zc = send(sq2.at[pl.ds(0, Z - 1)], sq2.at[pl.ds(0, Z - 1)], sq_s.at[1], sq_r.at[1], sib)
     all_zc = send(sq2, sq2, sq_s.at[1], sq_r.at[1], sib)
 
-    def send_xy(i, _):
-        to = place(lax.rem(y + i // X, Y), z, lax.rem(x + lax.rem(i, X), X), c)
-        send(sq1.at[0], sq1.at[i], sq_s.at[0], sq_r.at[0], to).start()
-        return 0
-
-    def send_zc(i, _):
-        to = place(y, lax.rem(z + Z // 2 + i // C, Z), x, lax.rem(c + 1 + lax.rem(i, C), C))
-
-        @pl.when(i != Z + 1)
-        def _():
+    def far_first(places):
+        return sorted(places, key=lambda steps: -sum(min(k, size - k) for k, size in zip(steps, (Y, Z, X, C))))
+
+    def send_xy():
+        for i, (dy, _, dx, _) in enumerate(far_first([(dy, 0, dx, 0) for dy in range(Y) for dx in range(X)])[:-1]):
+            to = place(lax.rem(y + dy, Y), z, lax.rem(x + dx, X), c)
+            send(sq1.at[0], sq1.at[1 + i], sq_s.at[0], sq_r.at[0], to).start()
+
+    def send_zc():
+        for _, dz, _, dc in far_first([(0, dz, 0, dc) for dz in range(Z) for dc in range(C)])[:-1]:
+            to = place(y, lax.rem(z + dz, Z), x, lax.rem(c + dc, C))
             send(sq2.at[z], sq2.at[z], sq_s.at[1], sq_r.at[1], to).start()
-
-        return 0
 
     @pl.when(taker)
     def _():
@@ -374,16 +373,14 @@
             squares += jnp.sum(total * total, axis=0, keepdims=True)
         cp_w.start()
         sq1[0] = squares
-        lax.fori_loop(1, Y * X, send_xy, 0)
+        send_xy()
         all_xy.wait_recv()
         sq2[z] = jnp.sum(sq1[...], axis=0)
-        lax.fori_loop(0, Z * C, send_zc, 0)
-        some_zc.wait_recv()
+        send_zc()
 
     @pl.when(jnp.logical_not(taker))
     def _():
         cp_w.wait_recv()
-        all_zc.wait_recv()
 
     def sums_left():
         @pl.when(taker)
@@ -398,13 +395,15 @@
     for k in range(C):
         at, then = pl.ds(k * ROWS, ROWS), pl.ds(PAIR + k * ROWS, ROWS)
         halves.append(jnp.concatenate([wsum[then, :], wsum[at, :]], axis=1))
-    rows_sum = jnp.where(c == 0, halves[0], halves[1])
+    w_ref[...] = jnp.where(c == 0, halves[0], halves[1])
+    pl.when(taker)(some_zc.wait_recv)
+    pl.when(jnp.logical_not(taker))(all_zc.wait_recv)
 
     lanes = jnp.sum(sq2[...], axis=0)
     square_total = jnp.sum(lanes, axis=1, keepdims=True)
     limit = math.sqrt(D * 2 * HD)
     clip = jnp.minimum(1.0, limit / (jnp.sqrt(square_total) + 1e-6))
-    w_ref[...] = rows_sum * clip
+    w_ref[...] *= clip
 
     for copy in [cp_q, cp_do, cp_st, *cp_k, *cp_v, *cp_x, *cp_ret, cp_dq, *cp_g]:
         copy.wait_send()

time: 48 us -> 48 us (level)
  no operation moved by 1% of the time
where the time goes in v7:
time: 48 us; the launch traced here: 47.9 us
  Pallas kernels  46 us (96%)
  local copies, waits for them, and re-layouts  1.28 us (3%)
  between operations  0.64 us (1%)
    pallas_call x1, Pallas kernels, on_device(): pl.pallas_call(kernel, out_shape=(pltpu.VMEM((ROWS, 2 * HD), f32), pltpu....  46 us
    unnamed x2, local copies, waits for them, and re-layouts  1.28 us

profile of v7, /device:TPU:1, one launch (start us, length us, event | category | flops | bytes accessed | tf_op | source)
XLA Modules:
  0.0 47.9 jit_solution(9621579268821736227)
XLA Ops:
  0.6 46.0 %clip_attention_backward.1 = (f32[20,256]{1,0:T(8,128)S(1)}, bf16[128,640]{1,0:T(8,128)(2,1)S(1)}) custom-call(bf16[128,640]{1,0:T(8,128)(2,1)} %q_hbm.1, bf16[128,128]{1,0:T(8,128)(2,1)} %k_hbm.1, bf16[128,128]{1,0:T(8,128)(2,1)} %v_hbm.1, bf16[128,640]{1,0:T(8,128)(2,1)} %o_hbm.1, bf16[128,640]{1,0:T(8,128)(2,1)} %do_hbm.1, f32[5,128]{1,0:T(8,128)} %lse_hbm.1, ...), custom_call_target="tpu_custom_call" | custom-call | tf_op jit(solution)/shard_map/clip_attention_backward/pallas_call | solution.py:418
  46.6 0.6 %copy.13 = f32[20,256]{1,0:T(8,128)} copy(f32[20,256]{1,0:T(8,128)S(1)} %get-tuple-element.2) | data formatting | bytes 40960
  47.3 0.7 %copy.14 = bf16[128,640]{1,0:T(8,128)(2,1)} copy(bf16[128,640]{1,0:T(8,128)(2,1)S(1)} %get-tuple-element.3) | data formatting | bytes 327680

commit v8 on v7

--- a/solution.py
+++ b/solution.py
@@ -168,7 +168,7 @@
         [send(src, buf.at[j], kv_s.at[2 * n + j - 1], kv_r.at[2 * n + j - 1], block_at(2 * j)) for j in (1, 2)]
         for n, (src, buf) in enumerate(((k_hbm, kbuf), (v_hbm, vbuf)))
     ]
-    for copy in [*cp_k, cp_q, cp_do, *cp_v]:
+    for copy in [*cp_k, *cp_v, cp_q, cp_do]:
         copy.start()
 
     def x_cols(yy, zz, cc):
@@ -254,7 +254,7 @@
         return part
 
     def give_back(n, part):
-        for j in (2, 1):
+        for j in (1, 2):
             k = 2 * n + j - 1
             ret_send[k] = part[(j - 1) * T : j * T].astype(bf16)
             copy = send(ret_send.at[k], ret_recv.at[k], ret_s.at[k], ret_r.at[k], block_at(-2 * j))

time: 48 us -> 47.8 us (level)
  no operation moved by 1% of the time
where the time goes in v8:
time: 47.8 us
  Pallas kernels  45.8 us (96%)
  local copies, waits for them, and re-layouts  1.28 us (3%)
  between operations  0.64 us (1%)
    pallas_call x1, Pallas kernels, on_device(): pl.pallas_call(kernel, out_shape=(pltpu.VMEM((ROWS, 2 * HD), f32), pltpu....  45.8 us
    unnamed x2, local copies, waits for them, and re-layouts  1.28 us

profile of v8, /device:TPU:1, one launch (start us, length us, event | category | flops | bytes accessed | tf_op | source)
XLA Modules:
  0.0 47.8 jit_solution(13077557025632846347)
XLA Ops:
  0.6 45.8 %clip_attention_backward.1 = (f32[20,256]{1,0:T(8,128)S(1)}, bf16[128,640]{1,0:T(8,128)(2,1)S(1)}) custom-call(bf16[128,640]{1,0:T(8,128)(2,1)} %q_hbm.1, bf16[128,128]{1,0:T(8,128)(2,1)} %k_hbm.1, bf16[128,128]{1,0:T(8,128)(2,1)} %v_hbm.1, bf16[128,640]{1,0:T(8,128)(2,1)} %o_hbm.1, bf16[128,640]{1,0:T(8,128)(2,1)} %do_hbm.1, f32[5,128]{1,0:T(8,128)} %lse_hbm.1, ...), custom_call_target="tpu_custom_call" | custom-call | tf_op jit(solution)/shard_map/clip_attention_backward/pallas_call | solution.py:418
  46.5 0.6 %copy.13 = f32[20,256]{1,0:T(8,128)} copy(f32[20,256]{1,0:T(8,128)S(1)} %get-tuple-element.2) | data formatting | bytes 40960
  47.1 0.7 %copy.14 = bf16[128,640]{1,0:T(8,128)(2,1)} copy(bf16[128,640]{1,0:T(8,128)(2,1)S(1)} %get-tuple-element.3) | data formatting | bytes 327680
